TPU v7x, 128 devices: a whole 4x4x4 slice. The times are simulated.
128 devices in a mesh: tile: 8 (over x, core), sweep: 16 (over z, y).
Axes of the slice: x: 4, y: 4, z: 4, core: 2. Of those that a mesh axis runs over, the one named last changes fastest.
Arguments:
- map_tiles: bfloat16 [128, 128, 512], P('tile'), may hold values from -6 to 6
- sweeps: bfloat16 [2, 128, 512, 512], P(None, ('tile', 'sweep')), may hold values from -6 to 6
- cotangents: bfloat16 [2, 128, 2, 512, 512], P(None, ('tile', 'sweep')), may hold values from -1.5 to 1.5
- offsets: int32 [2, 8], replicated, may hold values from 0 to 124
- turn_counts: int32 [2, 128, 2], P(None, ('tile', 'sweep')), may hold values from 0 to 3
Outputs:
- grad_map: float32 [128, 128, 512], P('tile', 'sweep')
- grad_sweeps: float32 [2, 128, 512, 512], P(None, ('tile', 'sweep'))
All inputs are finite; a program needn't handle non-finite values.
Results may differ from a plain program's by a relative error of at most 0.013.
Values may be sent and summed in bfloat16 or wider, within the bound.
No kernel may reach another device: no remote copies, remote signals or barrier semaphores. Data moves between devices by JAX's collectives and lax.ppermute only.
A program may use at most 128 MiB of HBM per device.

v0:
```python
from functools import partial
import math

import jax
import jax.numpy as jnp
import ml_dtypes
import numpy as np
from jax import lax
from jax.experimental import pallas as pl
from jax.experimental.pallas import tpu as pltpu
from jax.sharding import PartitionSpec as P

BF = jnp.bfloat16
F32 = jnp.float32
NT = (((1,), (1,)), ((), ()))


def flipped(even, odd, axis):
    return np.flip(even, axis), -np.flip(odd, axis)


def make_tables(side, order):
    half, quarter = side // 2, side // 4
    factor = 1.0 / math.sqrt(side)
    n = np.arange(half)
    alternating = np.where(n % 2 == 0, factor, -factor)

    def cs(n_ids, k_ids):
        angle = (np.outer(n_ids, k_ids) % side) * (2.0 * math.pi / side)
        return np.cos(angle) * factor, np.sin(angle) * factor

    low_even = 2 * np.arange(quarter)
    low_odd = low_even + 1
    all_even = 2 * np.arange(half)
    all_odd = all_even + 1
    c, s = cs(low_even, n)
    s[0] = -alternating
    down_e = np.concatenate([c, -s], 0)
    c, s = cs(low_odd, n)
    down_o = np.concatenate([c, -s], 0)
    across_e = np.concatenate(cs(n, all_even), 1)
    across_o = np.concatenate(cs(n, all_odd), 1)
    c, s = cs(n, low_even)
    s[:, 0] = -0.5 * alternating
    c[:, 0] *= 0.5
    up_e = 2.0 * np.concatenate([c, -s], 1)
    c, s = cs(n, low_odd)
    up_o = 2.0 * np.concatenate([c, -s], 1)

    def back_across(reverse):
        out = []
        for ids, sign in ((all_even, 1.0), (all_odd, -1.0)):
            parts = cs(ids, n)
            if reverse:
                parts = [np.flip(p, 1) * sign for p in parts]
            out.append(np.concatenate(parts, 1))
        return np.stack(out)

    def cast(x):
        return jnp.asarray(np.asarray(x, np.float32).astype(ml_dtypes.bfloat16))

    down = np.stack([np.stack([down_e, down_o]), np.stack(flipped(down_e, down_o, 1))])
    across = np.stack([np.stack([across_e, across_o]), np.stack(flipped(across_e, across_o, 0))])
    back = np.stack([back_across(False), back_across(True)])
    up = np.stack([np.stack([up_e, up_o]), np.stack(flipped(up_e, up_o, 0))])
    up_sent = np.stack([up_e[order], up_o[order]])
    return cast(down), cast(across), cast(back), cast(up), cast(up_sent)


def mm(a, b, dims=(((1,), (0,)), ((), ()))):
    return lax.dot_general(a, b, dims, preferred_element_type=F32)


def fold_columns(product):
    half = product.shape[1] // 2
    left, right = product[:, :half], product[:, half:]
    return (left + right).astype(BF), (left - right).astype(BF)


def row_pass(field, down, flip, plus, minus):
    half = plus.shape[1]
    top, bottom = field
    for parity, folded in ((0, top + bottom), (1, top - bottom)):
        p, m = fold_columns(mm(down[flip, parity], folded))
        plus[parity * half : (parity + 1) * half] = p
        minus[parity * half : (parity + 1) * half] = m


def row_pass_turned(field, down, flip, plus, minus):
    half = plus.shape[1]
    left, right = field[:, :half], field[:, half:]
    for parity, folded in ((0, left + right), (1, left - right)):
        p, m = fold_columns(mm(down[flip, parity], folded, NT))
        plus[parity * half : (parity + 1) * half] = p
        minus[parity * half : (parity + 1) * half] = m


def column_pass(plus, minus, across, flip, store, store_extra):
    half = plus.shape[1]
    quarter = half // 2
    for col, folded in ((0, plus), (1, minus)):
        table = across[flip, col]
        for row in (0, 1):
            both = mm(folded[row * half : (row + 1) * half], table)
            ea, fa = both[:quarter, :half], both[:quarter, half:]
            eb, fb = both[quarter:, :half], both[quarter:, half:]
            if row == 0:
                store_extra(col, eb[:8], -fb[:8])
                first = lax.broadcasted_iota(jnp.int32, eb.shape, 0) == 0
                eb = jnp.where(first, 0.0, eb)
                fb = jnp.where(first, 0.0, fb)
            store(row, col, ea + fb, eb - fa)


def inverse(packed, back, back_flip, up, up_index, middle):
    half = packed.shape[1] // 2
    quarter = half // 2
    for row in (0, 1):
        rows = packed[row * half : (row + 1) * half]
        parts = []
        for col in (0, 1):
            both = mm(rows[:, col * half : (col + 1) * half], back[back_flip, col])
            ea, fa = both[:quarter, :half], both[:quarter, half:]
            eb, fb = both[quarter:, :half], both[quarter:, half:]
            parts.append((ea - fb, eb + fa))
        (re, ie), (ro, io) = parts
        base = row * half
        middle[base : base + quarter, :half] = (re + ro).astype(BF)
        middle[base : base + quarter, half:] = (re - ro).astype(BF)
        middle[base + quarter : base + half, :half] = (ie + io).astype(BF)
        middle[base + quarter : base + half, half:] = (ie - io).astype(BF)
    even = mm(up_index(up, 0), middle[:half])
    odd = mm(up_index(up, 1), middle[half:])
    return even + odd, even - odd


def blocks(half):
    quarter = half // 2
    for row in (0, 1):
        for col in (0, 1):
            real = (slice(row * half, row * half + quarter), slice(col * half, (col + 1) * half))
            imag = (slice(row * half + quarter, (row + 1) * half), real[1])
            yield row, col, real, imag


def merge_row(real, imag, extra_real, extra_imag):
    pad = jnp.zeros((real.shape[0] - 8, real.shape[1]), F32)
    first = lax.broadcasted_iota(jnp.int32, extra_real.shape, 0) == 0
    extra_real = jnp.concatenate([jnp.where(first, extra_real, 0.0), pad], 0)
    extra_imag = jnp.concatenate([jnp.where(first, extra_imag, 0.0), pad], 0)
    return real - extra_imag, imag + extra_real


def map_kernel(
    turns, sweep, cots, down, across, back, up_sent, spec, spec_extra, sent,
    plus, minus, swept, swept_extra, total, total_extra, packed, middle,
):
    q = pl.program_id(0)
    side = sweep.shape[1]
    half = side // 2

    for r in range(cots.shape[1]):
        turn = turns[q, r]
        flip_rows = ((turn == 1) | (turn == 2)).astype(jnp.int32)
        flip_cols = (turn >= 2).astype(jnp.int32)

        @pl.when(turn % 2 == 0)
        def _():
            row_pass((sweep[0, :half], sweep[0, half:]), down, flip_rows, plus, minus)

        @pl.when(turn % 2 == 1)
        def _():
            row_pass_turned(sweep.at[0], down, flip_rows, plus, minus)

        def keep(row, col, real, imag):
            rows = slice(row * (half // 2), (row + 1) * (half // 2))
            swept[0, rows, col * half : (col + 1) * half] = real
            swept[1, rows, col * half : (col + 1) * half] = imag

        def keep_extra(col, real, imag):
            swept_extra[0, :, col * half : (col + 1) * half] = real
            swept_extra[1, :, col * half : (col + 1) * half] = imag

        column_pass(plus, minus, across, flip_cols, keep, keep_extra)
        row_pass((cots[0, r, :half], cots[0, r, half:]), down, 0, plus, minus)

        def meet(row, col, real, imag):
            quarter = half // 2
            base = row * half
            cols = slice(col * half, (col + 1) * half)
            rows = slice(row * quarter, (row + 1) * quarter)
            spec[0, r, base : base + quarter, cols] = real.astype(BF)
            spec[0, r, base + quarter : base + half, cols] = imag.astype(BF)
            sr, si = swept[0, rows, cols], swept[1, rows, cols]
            tr, ti = real * sr - imag * si, real * si + imag * sr
            if r > 0:
                tr, ti = total[0, rows, cols] + tr, total[1, rows, cols] + ti
            if r < cots.shape[1] - 1:
                total[0, rows, cols] = tr
                total[1, rows, cols] = ti
            else:
                if row == 0:
                    tr, ti = merge_row(tr, ti, total_extra[0, :, cols], total_extra[1, :, cols])
                packed[base : base + quarter, cols] = tr.astype(BF)
                packed[base + quarter : base + half, cols] = ti.astype(BF)

        def meet_extra(col, real, imag):
            cols = slice(col * half, (col + 1) * half)
            spec_extra[0, r, 0, :, cols] = real
            spec_extra[0, r, 1, :, cols] = imag
            sr, si = swept_extra[0, :, cols], swept_extra[1, :, cols]
            tr, ti = real * sr - imag * si, real * si + imag * sr
            if r > 0:
                tr, ti = total_extra[0, :, cols] + tr, total_extra[1, :, cols] + ti
            total_extra[0, :, cols] = tr
            total_extra[1, :, cols] = ti

        column_pass(plus, minus, across, 0, meet, meet_extra)

    top, bottom = inverse(packed, back, 0, up_sent, lambda u, parity: u[parity], middle)
    parts = sent.shape[1]
    rows = half // parts
    sent[0, :, :rows] = top.astype(BF).reshape(parts, rows, side)
    sent[0, :, rows:] = bottom.astype(BF).reshape(parts, rows, side)


def sweep_kernel(
    turns, source, tiles, spec, spec_extra, down, across, back, up, out,
    plus, minus, window, window_extra, packed, middle, total,
):
    q = pl.program_id(0)
    side = out.shape[2]
    half = side // 2
    quarter = half // 2

    def tile(k):
        return tiles[source[q, k], 0]

    top = jnp.concatenate([tile(0), tile(1)], 0)
    bottom = jnp.concatenate([tile(2), tile(3)], 0)
    row_pass((top, bottom), down, 0, plus, minus)

    def keep(row, col, real, imag):
        rows = slice(row * quarter, (row + 1) * quarter)
        window[0, rows, col * half : (col + 1) * half] = real
        window[1, rows, col * half : (col + 1) * half] = imag

    def keep_extra(col, real, imag):
        window_extra[0, :, col * half : (col + 1) * half] = real
        window_extra[1, :, col * half : (col + 1) * half] = imag

    column_pass(plus, minus, across, 0, keep, keep_extra)
    total[...] = jnp.zeros_like(total)
    for r in range(spec.shape[1]):
        turn = turns[q, r]
        flip_rows = ((turn == 1) | (turn == 2)).astype(jnp.int32)
        flip_cols = (turn >= 2).astype(jnp.int32)
        for row, col, real, imag in blocks(half):
            rows = slice(row * quarter, (row + 1) * quarter)
            cols = real[1]
            gr, gi = spec[(0, r) + real].astype(F32), spec[(0, r) + imag].astype(F32)
            wr, wi = window[0, rows, cols], window[1, rows, cols]
            br, bi = gr * wr + gi * wi, gr * wi - gi * wr
            if row == 0:
                gr, gi = spec_extra[0, r, 0, :, cols], spec_extra[0, r, 1, :, cols]
                wr, wi = window_extra[0, :, cols], window_extra[1, :, cols]
                br, bi = merge_row(br, bi, gr * wr + gi * wi, gr * wi - gi * wr)
            packed[real] = br.astype(BF)
            packed[imag] = bi.astype(BF)
        top, bottom = inverse(
            packed, back, flip_cols, up, lambda u, parity: u[flip_rows, parity], middle
        )
        total[turn % 2, :half] += top
        total[turn % 2, half:] += bottom
    out[0, 0] = total[0] + total[1].T


def pick_kernel(wanted, tiles, out, sem):
    groups, rounds = out.shape[:2]
    copies = [
        pltpu.make_async_copy(tiles.at[wanted[q, i]], out.at[i, q], sem.at[q, i])
        for i in range(groups)
        for q in range(rounds)
    ]
    for copy in copies:
        copy.start()
    for copy in copies:
        copy.wait()


def spread_kernel(position, own, first, second, third, out):
    rounds = own.shape[0]
    groups, slots = position.shape[1], out.shape[1]
    share = out.shape[2] // rounds
    side = own.shape[2]
    summed = (
        own[...].astype(F32) + first[...].astype(F32) + second[...].astype(F32) + third[...].astype(F32)
    )
    span = own.shape[1] // (slots * share)
    summed = summed.reshape(rounds, span, slots, share, side)
    for i in range(groups):
        parts = []
        for q in range(rounds):
            part = jnp.zeros((slots, share, side), F32)
            for k in range(span):
                part = jnp.where(position[q, i] == k, summed[q, k], part)
            parts.append(part)
        out[i] = jnp.concatenate(parts, 1).astype(BF)


def gather_kernel(wanted, holding, incoming, out):
    rounds, groups = wanted.shape
    share = out.shape[1]
    out[...] = jnp.zeros_like(out)
    for i in range(groups):
        summed = jnp.sum(incoming[i].astype(F32), 0)
        for q in range(rounds):

            @pl.when(holding[q, i] == 1)
            def _():
                out[wanted[q, i]] += summed[q * share : (q + 1) * share]


def full(shape):
    return pl.BlockSpec(shape, lambda *_: (0,) * len(shape))


SMEM = pl.BlockSpec(memory_space=pltpu.SMEM)
VMEM = pl.BlockSpec(memory_space=pltpu.VMEM)
ANY = pl.BlockSpec(memory_space=pl.ANY)
PARAMS = pltpu.CompilerParams(vmem_limit_bytes=50 * 1024 * 1024)


def shards(map_tiles, sweeps, cotangents, offsets, turn_counts):
    groups = lax.axis_size("tile")
    members = lax.axis_size("sweep")
    own_group = lax.axis_index("tile")
    own_member = lax.axis_index("sweep")
    tile_rows, side = map_tiles.shape[1:]
    rounds = sweeps.shape[0]
    hypotheses = cotangents.shape[2]
    half = side // 2
    span = side // tile_rows
    share = tile_rows // members
    near = 4
    far = members // near
    turns = turn_counts[:, 0]
    sweeps = sweeps[:, 0]
    cotangents = cotangents[:, 0]

    order = (
        np.arange(half).reshape(span // 2, far, near, share).transpose(2, 0, 1, 3).reshape(-1)
    )
    down, across, back, up, up_sent = make_tables(side, order)

    peers = jnp.arange(groups, dtype=jnp.int32)
    step = (own_group - offsets) % groups
    holding = (step < span).astype(jnp.int32)
    wanted = jnp.where(step < span, (offsets + step) // groups, 0).astype(jnp.int32)
    own_start = lax.dynamic_slice_in_dim(offsets, own_group, 1, 1)
    source = ((own_start + jnp.arange(span, dtype=jnp.int32)) % groups).astype(jnp.int32)
    position = ((peers[None] - own_start) % groups).astype(jnp.int32)

    outgoing = pl.pallas_call(
        pick_kernel,
        out_shape=jax.ShapeDtypeStruct((groups, rounds, tile_rows, side), BF),
        in_specs=[SMEM, ANY],
        out_specs=ANY,
        scratch_shapes=[pltpu.SemaphoreType.DMA((rounds, groups))],
        name="pick",
    )(wanted, map_tiles)
    incoming = lax.all_to_all(outgoing, "tile", split_axis=0, concat_axis=0, tiled=True)

    unit = 2 * side**3
    spec, spec_extra, sent = pl.pallas_call(
        map_kernel,
        grid=(rounds,),
        out_shape=[
            jax.ShapeDtypeStruct((rounds, hypotheses, side, side), BF),
            jax.ShapeDtypeStruct((rounds, hypotheses, 2, 8, side), F32),
            jax.ShapeDtypeStruct((rounds, near, side // near, side), BF),
        ],
        in_specs=[
            SMEM,
            pl.BlockSpec((1, side, side), lambda q: (q, 0, 0)),
            pl.BlockSpec((1, hypotheses, side, side), lambda q: (q, 0, 0, 0)),
            full(down.shape),
            full(across.shape),
            full(back.shape),
            full(up_sent.shape),
        ],
        out_specs=[
            pl.BlockSpec((1, hypotheses, side, side), lambda q: (q, 0, 0, 0)),
            pl.BlockSpec((1, hypotheses, 2, 8, side), lambda q: (q, 0, 0, 0, 0)),
            pl.BlockSpec((1, near, side // near, side), lambda q: (q, 0, 0, 0)),
        ],
        scratch_shapes=[
            pltpu.VMEM((side, half), BF),
            pltpu.VMEM((side, half), BF),
            pltpu.VMEM((2, half, side), F32),
            pltpu.VMEM((2, 8, side), F32),
            pltpu.VMEM((2, half, side), F32),
            pltpu.VMEM((2, 8, side), F32),
            pltpu.VMEM((side, side), BF),
            pltpu.VMEM((side, side), BF),
        ],
        compiler_params=PARAMS,
        cost_estimate=pl.CostEstimate(
            flops=int(8 * rounds * unit), bytes_accessed=8 * 1024 * 1024, transcendentals=0
        ),
        name="map_terms",
    )(turns, sweeps, cotangents, down, across, back, up_sent)

    own_near = own_member % near
    received = [lax.dynamic_index_in_dim(sent, own_near, 1, keepdims=False)]
    for shift in range(1, near):
        target = (own_near + shift) % near
        block = lax.dynamic_index_in_dim(sent, target, 1, keepdims=False)
        pairs = [(m, m // near * near + (m + shift) % near) for m in range(members)]
        received.append(lax.ppermute(block, "sweep", pairs))

    spread = pl.pallas_call(
        spread_kernel,
        out_shape=jax.ShapeDtypeStruct((groups, far, rounds * share, side), BF),
        in_specs=[SMEM] + [VMEM] * near,
        out_specs=VMEM,
        compiler_params=PARAMS,
        name="spread",
    )(position, *received)
    index_groups = [
        [t * members + f * near + y for t in range(groups) for f in range(far)] for y in range(near)
    ]
    spread = spread.reshape(groups * far, rounds * share, side)
    landed = lax.all_to_all(
        spread,
        ("tile", "sweep"),
        split_axis=0,
        concat_axis=0,
        tiled=True,
        axis_index_groups=index_groups,
    )
    grad_map = pl.pallas_call(
        gather_kernel,
        out_shape=jax.ShapeDtypeStruct((map_tiles.shape[0], share, side), F32),
        in_specs=[SMEM, SMEM, VMEM],
        out_specs=VMEM,
        compiler_params=PARAMS,
        name="gather",
    )(wanted, holding, landed.reshape(groups, far, rounds * share, side))

    grad_sweeps = pl.pallas_call(
        sweep_kernel,
        grid=(rounds,),
        out_shape=jax.ShapeDtypeStruct((rounds, 1, side, side), F32),
        in_specs=[
            SMEM,
            SMEM,
            pl.BlockSpec((groups, 1, tile_rows, side), lambda q: (0, q, 0, 0)),
            pl.BlockSpec((1, hypotheses, side, side), lambda q: (q, 0, 0, 0)),
            pl.BlockSpec((1, hypotheses, 2, 8, side), lambda q: (q, 0, 0, 0, 0)),
            full(down.shape),
            full(across.shape),
            full(back.shape),
            full(up.shape),
        ],
        out_specs=pl.BlockSpec((1, 1, side, side), lambda q: (q, 0, 0, 0)),
        scratch_shapes=[
            pltpu.VMEM((side, half), BF),
            pltpu.VMEM((side, half), BF),
            pltpu.VMEM((2, half, side), F32),
            pltpu.VMEM((2, 8, side), F32),
            pltpu.VMEM((side, side), BF),
            pltpu.VMEM((side, side), BF),
            pltpu.VMEM((2, side, side), F32),
        ],
        compiler_params=PARAMS,
        cost_estimate=pl.CostEstimate(
            flops=int(5 * rounds * unit), bytes_accessed=8 * 1024 * 1024, transcendentals=0
        ),
        name="sweep_terms",
    )(turns, source, incoming, spec, spec_extra, down, across, back, up)
    return grad_map, grad_sweeps


def solution(mesh):
    in_specs = (
        P("tile", None, None),
        P(None, ("tile", "sweep"), None, None),
        P(None, ("tile", "sweep"), None, None, None),
        P(),
        P(None, ("tile", "sweep"), None),
    )
    out_specs = (P("tile", "sweep", None), P(None, ("tile", "sweep"), None, None))
    return jax.shard_map(shards, mesh=mesh, in_specs=in_specs, out_specs=out_specs, check_vma=False)
```

profile of v0, /device:TPU:1, one launch (start us, length us, event | category | flops | bytes accessed | tf_op | source)
XLA Modules:
  0.0 147.5 jit_solution(15929988808537757417)
XLA Ops:
  0.7 0.0 copy-start.1
  0.7 1.2 copy-done.1
  1.9 0.0 copy-start.2
  1.9 0.7 copy-done.2
  2.6 0.0 copy-start.4
  2.6 1.2 copy-done.4
  3.8 0.0 copy-start.7
  3.8 1.0 copy-done.7
  4.9 0.0 copy-start.10
  4.9 0.9 copy-done.10
  5.8 8.3 %map_terms.1 = (bf16[2,2,512,512]{3,2,1,0:T(8,128)(2,1)}, f32[2,2,2,8,512]{4,3,2,1,0:T(8,128)S(1)}, bf16[2,4,128,512]{3,2,1,0:T(8,128)(2,1)S(1)}) custom-call(s32[2,2]{1,0:T(2,128)S(1)} %bitcast.15, bf16[2,512,512]{2,1,0:T(8,128)(2,1)S(1)} %bitcast.14, bf16[2,2,512,512]{3,2,1,0:T(8,128)(2,1)} %bitcast.17, bf16[2,2,256,256]{3,2,1,0:T(8,128)(2,1)S(1)} %copy-done.7, ...), custom_call_target="tpu_custom_call" | custom-call | flops 4294967296 | bytes 8388608 | tf_op jit(solution)/shard_map/map_terms/pallas_call | solution.py:375
  14.1 0.0 copy-start.11
  14.1 0.1 dynamic-slice_bitcast_fusion
  14.2 2.2 %collective-permute-start = (bf16[2,128,512]{2,1,0:T(8,128)(2,1)S(1)}, bf16[2,128,512]{2,1,0:T(8,128)(2,1)S(1)}, u32[]{:S(2)}, u32[]{:S(2)}) collective-permute-start(bf16[2,128,512]{2,1,0:T(8,128)(2,1)S(1)} %get-tuple-element.12), channel_id=1, source_target_pairs={{0,1},{1,2},{2,3},{3,0},{4,5},{5,6},{6,7},{7,4},{8,9},{9,10},{10,1... | collective-permute-start | bytes 786440 | tf_op jit(solution)/shard_map/ppermute | solution.py:420
  16.5 2.6 %collective-permute-start.1 = (bf16[2,128,512]{2,1,0:T(8,128)(2,1)S(1)}, bf16[2,128,512]{2,1,0:T(8,128)(2,1)S(1)}, u32[]{:S(2)}, u32[]{:S(2)}) collective-permute-start(bf16[2,128,512]{2,1,0:T(8,128)(2,1)S(1)} %get-tuple-element.11), channel_id=1, source_target_pairs={{0,2},{1,3},{2,0},{3,1},{4,6},{5,7},{6,4},{7,5},{8,10},{9,11},{10,... | collective-permute-start | bytes 786440 | tf_op jit(solution)/shard_map/ppermute | solution.py:420
  19.1 1.0 collective-permute-start.2
  20.1 0.0 copy-done.11
  20.1 0.2 fusion
  20.3 0.1 and_select_fusion.1.position
  20.4 3.5 %collective-permute-done.first = bf16[2,128,512]{2,1,0:T(8,128)(2,1)S(1)} collective-permute-done((bf16[2,128,512]{2,1,0:T(8,128)(2,1)S(1)}, bf16[2,128,512]{2,1,0:T(8,128)(2,1)S(1)}, u32[]{:S(2)}, u32[]{:S(2)}) %collective-permute-start) | collective-permute-done | bytes 262176 | tf_op jit(solution)/shard_map/ppermute | solution.py:420
  23.9 6.6 %collective-permute-done.1.second = bf16[2,128,512]{2,1,0:T(8,128)(2,1)S(1)} collective-permute-done((bf16[2,128,512]{2,1,0:T(8,128)(2,1)S(1)}, bf16[2,128,512]{2,1,0:T(8,128)(2,1)S(1)}, u32[]{:S(2)}, u32[]{:S(2)}) %collective-permute-start.1) | collective-permute-done | bytes 262176 | tf_op jit(solution)/shard_map/ppermute | solution.py:420
  30.5 0.0 collective-permute-done.2.third
  30.5 1.6 %spread.1 = bf16[8,4,16,512]{3,2,1,0:T(8,128)(2,1)} custom-call(s32[2,8]{1,0:T(2,128)S(1)} %and_select_fusion.1.position, bf16[2,128,512]{2,1,0:T(8,128)(2,1)S(1)} %get-tuple-element.13.own, bf16[2,128,512]{2,1,0:T(8,128)(2,1)S(1)} %collective-permute-done.first, bf16[2,128,512]{2,1,0:T(8,128)(2,1)S(1)} %collective-permute-done.1.second, ...), custom_call_target="tpu_custom_call" | custom-call | tf_op jit(solution)/shard_map/spread/pallas_call | solution.py:422
  32.1 9.4 %all-to-all-start = ((bf16[32,16,512]{2,1,0:T(8,128)(2,1)}), bf16[32,16,512]{2,1,0:T(8,128)(2,1)S(1)}, u32[]{:S(2)}, u32[]{:S(2)}) async-start(bf16[32,16,512]{2,1,0:T(8,128)(2,1)} %bitcast.7), calls=%async_computation | async-start | bytes 1048576 | tf_op jit(solution)/shard_map/all_to_all | solution.py:434
  41.6 0.6 fusion.4.wanted
  42.1 65.5 %pick.1 = bf16[8,2,128,512]{3,2,1,0:T(8,128)(2,1)} custom-call(s32[2,8]{1,0:T(2,128)} %fusion.4.wanted, bf16[16,128,512]{2,1,0:T(8,128)(2,1)} %tiles.1), custom_call_target="tpu_custom_call" | custom-call | tf_op jit(solution)/shard_map/pick/pallas_call | solution.py:364
  107.6 0.0 copy-start
  107.6 0.0 copy-start.3
  107.6 0.0 copy-start.5
  107.6 0.0 copy-start.6
  107.7 0.0 copy-start.8
  107.7 0.0 all-to-all-done
  107.7 5.0 %all-to-all-start.1 = ((bf16[8,2,128,512]{3,2,1,0:T(8,128)(2,1)}), bf16[8,2,128,512]{3,2,1,0:T(8,128)(2,1)}, u32[]{:S(2)}, u32[]{:S(2)}) async-start(bf16[8,2,128,512]{3,2,1,0:T(8,128)(2,1)} %pick.1), calls=%async_computation.1 | async-start | bytes 4194304 | tf_op jit(solution)/shard_map/all_to_all | solution.py:372
  112.6 0.1 and_select_fusion.source
  112.7 0.0 copy-done
  112.7 1.4 gather.1
  114.1 24.9 %all-to-all-done.1.tiles = bf16[8,2,128,512]{3,2,1,0:T(8,128)(2,1)} async-done(((bf16[8,2,128,512]{3,2,1,0:T(8,128)(2,1)}), bf16[8,2,128,512]{3,2,1,0:T(8,128)(2,1)}, u32[]{:S(2)}, u32[]{:S(2)}) %all-to-all-start.1) | async-done | bytes 2097184 | tf_op jit(solution)/shard_map/all_to_all | solution.py:372
  139.1 0.0 copy-done.3
  139.1 0.0 copy-done.5
  139.1 0.0 copy-done.6
  139.1 0.0 copy-done.8
  139.1 0.0 copy-start.9
  139.1 1.0 copy-done.9
  140.1 7.4 %sweep_terms.1 = f32[2,1,512,512]{3,2,1,0:T(8,128)} custom-call(s32[2,2]{1,0:T(2,128)S(1)} %bitcast.16, s32[2,4]{1,0:T(2,128)S(1)} %and_select_fusion.source, bf16[8,2,128,512]{3,2,1,0:T(8,128)(2,1)} %all-to-all-done.1.tiles, bf16[2,2,512,512]{3,2,1,0:T(8,128)(2,1)} %get-tuple-element.6.spec, f32[2,2,2,8,512]{4,3,2,1,0:T(8,128)S(1)} %get-tuple-element.7.spec_extra, ...), custom_call_target="tpu_custom_call" | custom-call | flops 2684354560 | bytes 8388608 | tf_op jit(solution)/shard_map/sweep_terms/pallas_call | solution.py:451
  (1 shorter events, 0.0 us)
Async XLA Ops:
  0.7 1.2 copy-start.1
  1.9 0.7 copy-start.2
  2.6 1.2 copy-start.4
  3.8 1.0 copy-start.7
  4.9 0.9 copy-start.10
  14.1 6.0 %copy-start.11 = (s32[2,8]{1,0:T(2,128)S(1)}, s32[2,8]{1,0:T(2,128)}, u32[]{:S(2)}) copy-start(s32[2,8]{1,0:T(2,128)} %param.13) | copy-start | bytes 196
  14.2 9.6 %collective-permute-start = (bf16[2,128,512]{2,1,0:T(8,128)(2,1)S(1)}, bf16[2,128,512]{2,1,0:T(8,128)(2,1)S(1)}, u32[]{:S(2)}, u32[]{:S(2)}) collective-permute-start(bf16[2,128,512]{2,1,0:T(8,128)(2,1)S(1)} %get-tuple-element.12), channel_id=1, source_target_pairs={{0,1},{1,2},{2,3},{3,0},{4,5},{5,6},{6,7},{7,4},{8,9},{9,10},{10,1... | collective-permute-start | bytes 786440 | tf_op jit(solution)/shard_map/ppermute | solution.py:420
  16.5 14.0 %collective-permute-start.1 = (bf16[2,128,512]{2,1,0:T(8,128)(2,1)S(1)}, bf16[2,128,512]{2,1,0:T(8,128)(2,1)S(1)}, u32[]{:S(2)}, u32[]{:S(2)}) collective-permute-start(bf16[2,128,512]{2,1,0:T(8,128)(2,1)S(1)} %get-tuple-element.11), channel_id=1, source_target_pairs={{0,2},{1,3},{2,0},{3,1},{4,6},{5,7},{6,4},{7,5},{8,10},{9,11},{10,... | collective-permute-start | bytes 786440 | tf_op jit(solution)/shard_map/ppermute | solution.py:420
  19.1 11.4 %collective-permute-start.2 = (bf16[2,128,512]{2,1,0:T(8,128)(2,1)S(1)}, bf16[2,128,512]{2,1,0:T(8,128)(2,1)S(1)}, u32[]{:S(2)}, u32[]{:S(2)}) collective-permute-start(bf16[2,128,512]{2,1,0:T(8,128)(2,1)S(1)} %get-tuple-element.10), channel_id=1, source_target_pairs={{0,3},{1,0},{2,1},{3,2},{4,7},{5,4},{6,5},{7,6},{8,11},{9,8},{10,9... | collective-permute-start | bytes 786440 | tf_op jit(solution)/shard_map/ppermute | solution.py:420
  32.1 75.5 %all-to-all-start = ((bf16[32,16,512]{2,1,0:T(8,128)(2,1)}), bf16[32,16,512]{2,1,0:T(8,128)(2,1)S(1)}, u32[]{:S(2)}, u32[]{:S(2)}) async-start(bf16[32,16,512]{2,1,0:T(8,128)(2,1)} %bitcast.7), calls=%async_computation | async-start | bytes 1048576 | tf_op jit(solution)/shard_map/all_to_all | solution.py:434
  107.6 5.1 %copy-start = (s32[2,8]{1,0:T(2,128)S(1)}, s32[2,8]{1,0:T(2,128)}, u32[]{:S(2)}) copy-start(s32[2,8]{1,0:T(2,128)} %fusion.4.wanted) | copy-start | bytes 196
  107.6 31.5 %copy-start.3 = (s32[2,1,2]{2,1,0:T(1,128)S(1)}, s32[2,1,2]{2,1,0:T(1,128)}, u32[]{:S(2)}) copy-start(s32[2,1,2]{2,1,0:T(1,128)} %param.14) | copy-start | bytes 52
  107.6 31.4 %copy-start.5 = (bf16[2,2,256,512]{3,2,1,0:T(8,128)(2,1)S(1)}, bf16[2,2,256,512]{3,2,1,0:T(8,128)(2,1)}, u32[]{:S(2)}) copy-start(bf16[2,2,256,512]{3,2,1,0:T(8,128)(2,1)} %constant.100.clone.across) | copy-start | bytes 3145732
  107.6 31.4 %copy-start.6 = (bf16[2,2,256,512]{3,2,1,0:T(8,128)(2,1)S(1)}, bf16[2,2,256,512]{3,2,1,0:T(8,128)(2,1)}, u32[]{:S(2)}) copy-start(bf16[2,2,256,512]{3,2,1,0:T(8,128)(2,1)} %constant.101.clone.back) | copy-start | bytes 3145732
  107.7 31.4 %copy-start.8 = (bf16[2,2,256,256]{3,2,1,0:T(8,128)(2,1)S(1)}, bf16[2,2,256,256]{3,2,1,0:T(8,128)(2,1)}, u32[]{:S(2)}) copy-start(bf16[2,2,256,256]{3,2,1,0:T(8,128)(2,1)} %constant.99.clone.down) | copy-start | bytes 1572868
  107.7 31.4 %all-to-all-start.1 = ((bf16[8,2,128,512]{3,2,1,0:T(8,128)(2,1)}), bf16[8,2,128,512]{3,2,1,0:T(8,128)(2,1)}, u32[]{:S(2)}, u32[]{:S(2)}) async-start(bf16[8,2,128,512]{3,2,1,0:T(8,128)(2,1)} %pick.1), calls=%async_computation.1 | async-start | bytes 4194304 | tf_op jit(solution)/shard_map/all_to_all | solution.py:372
  139.1 1.0 copy-start.9
where the time goes:
time: 148 us
  Pallas kernels  84.2 us (57%)
  waiting for transfers between devices  35 us (24%)
  starting transfers between devices  20.2 us (14%)
  local copies, waits for them, and re-layouts  6.47 us (4%)
    pallas_call x1, Pallas kernels, shards(): pl.pallas_call(pick_kernel, out_shape=jax.ShapeDtypeStruct((groups, round...  65.5 us
    all_to_all x1, waiting for transfers between devices, shards(): lax.all_to_all(outgoing, 'tile', split_axis=0, concat_axis=0, tiled=True)  24.9 us
    ppermute x3, waiting for transfers between devices, shards(): received.append(lax.ppermute(block, 'sweep', pairs))  10.1 us
    all_to_all x1, starting transfers between devices, shards(): lax.all_to_all(spread, ('tile', 'sweep'), split_axis=0, concat_axis=0, ti...  9.39 us
    pallas_call x1, Pallas kernels, shards(): pl.pallas_call(map_kernel, grid=(rounds,), out_shape=[jax.ShapeDtypeStruc...  8.29 us
    pallas_call x1, Pallas kernels, shards(): pl.pallas_call(sweep_kernel, grid=(rounds,), out_shape=jax.ShapeDtypeStru...  7.38 us
    unnamed x24, local copies, waits for them, and re-layouts  6.19 us
    ppermute x3, starting transfers between devices, shards(): received.append(lax.ppermute(block, 'sweep', pairs))  5.9 us
  transfers between devices with their start and end apart: 5, of which 3 were waited for; matrix products, arithmetic and copies ran while one was open for 1% of the time, Pallas kernels for 45%

commit v1 on v0

--- a/solution.py
+++ b/solution.py
@@ -19,7 +19,7 @@
     return np.flip(even, axis), -np.flip(odd, axis)
 
 
-def make_tables(side, order):
+def make_tables(side, order, near):
     half, quarter = side // 2, side // 4
     factor = 1.0 / math.sqrt(side)
     n = np.arange(half)
@@ -63,7 +63,7 @@
     across = np.stack([np.stack([across_e, across_o]), np.stack(flipped(across_e, across_o, 0))])
     back = np.stack([back_across(False), back_across(True)])
     up = np.stack([np.stack([up_e, up_o]), np.stack(flipped(up_e, up_o, 0))])
-    up_sent = np.stack([up_e[order], up_o[order]])
+    up_sent = np.stack([up_e[order], up_o[order]]).reshape(2, near, half // near, half)
     return cast(down), cast(across), cast(back), cast(up), cast(up_sent)
 
 
@@ -151,16 +151,25 @@
     return real - extra_imag, imag + extra_real
 
 
+def members_of(near):
+    member = lax.axis_index("sweep")
+    return member // near, member % near
+
+
 def map_kernel(
-    turns, sweep, cots, down, across, back, up_sent, spec, spec_extra, sent,
-    plus, minus, swept, swept_extra, total, total_extra, packed, middle,
+    turns, sweep, cots, down, across, back, up_sent, spec, spec_extra, *rest
 ):
     q = pl.program_id(0)
+    near = up_sent.shape[1]
+    sent, rest = rest[:near], rest[near:]
+    plus, minus, swept, swept_extra, total, total_extra, packed, middle = rest
     side = sweep.shape[1]
     half = side // 2
-
-    for r in range(cots.shape[1]):
-        turn = turns[q, r]
+    quarter = half // 2
+    hypotheses = cots.shape[1]
+
+    for r in range(hypotheses):
+        turn = turns[q, 0, r]
         flip_rows = ((turn == 1) | (turn == 2)).astype(jnp.int32)
         flip_cols = (turn >= 2).astype(jnp.int32)
 
@@ -173,7 +182,7 @@
             row_pass_turned(sweep.at[0], down, flip_rows, plus, minus)
 
         def keep(row, col, real, imag):
-            rows = slice(row * (half // 2), (row + 1) * (half // 2))
+            rows = slice(row * quarter, (row + 1) * quarter)
             swept[0, rows, col * half : (col + 1) * half] = real
             swept[1, rows, col * half : (col + 1) * half] = imag
 
@@ -185,7 +194,6 @@
         row_pass((cots[0, r, :half], cots[0, r, half:]), down, 0, plus, minus)
 
         def meet(row, col, real, imag):
-            quarter = half // 2
             base = row * half
             cols = slice(col * half, (col + 1) * half)
             rows = slice(row * quarter, (row + 1) * quarter)
@@ -195,7 +203,7 @@
             tr, ti = real * sr - imag * si, real * si + imag * sr
             if r > 0:
                 tr, ti = total[0, rows, cols] + tr, total[1, rows, cols] + ti
-            if r < cots.shape[1] - 1:
+            if r < hypotheses - 1:
                 total[0, rows, cols] = tr
                 total[1, rows, cols] = ti
             else:
@@ -217,27 +225,36 @@
 
         column_pass(plus, minus, across, 0, meet, meet_extra)
 
-    top, bottom = inverse(packed, back, 0, up_sent, lambda u, parity: u[parity], middle)
-    parts = sent.shape[1]
-    rows = half // parts
-    sent[0, :, :rows] = top.astype(BF).reshape(parts, rows, side)
-    sent[0, :, rows:] = bottom.astype(BF).reshape(parts, rows, side)
+    _, own = members_of(near)
+    ahead = [(own + shift) % near for shift in range(near)]
+
+    def up_index(table, parity):
+        return jnp.concatenate([table[parity, y] for y in ahead], 0)
+
+    top, bottom = inverse(packed, back, 0, up_sent, up_index, middle)
+    top, bottom = top.astype(BF), bottom.astype(BF)
+    rows = half // near
+    for shift in range(near):
+        sent[shift][0, :rows] = top[shift * rows : (shift + 1) * rows]
+        sent[shift][0, rows:] = bottom[shift * rows : (shift + 1) * rows]
 
 
 def sweep_kernel(
-    turns, source, tiles, spec, spec_extra, down, across, back, up, out,
+    offsets, turns, tiles, spec, spec_extra, down, across, back, up, out,
     plus, minus, window, window_extra, packed, middle, total,
 ):
     q = pl.program_id(0)
     side = out.shape[2]
     half = side // 2
     quarter = half // 2
+    groups, _, tile_rows, _ = tiles.shape
+    start = offsets[q, lax.axis_index("tile")]
 
     def tile(k):
-        return tiles[source[q, k], 0]
-
-    top = jnp.concatenate([tile(0), tile(1)], 0)
-    bottom = jnp.concatenate([tile(2), tile(3)], 0)
+        return tiles[(start + k) % groups, 0]
+
+    top = jnp.concatenate([tile(k) for k in range(half // tile_rows)], 0)
+    bottom = jnp.concatenate([tile(k + half // tile_rows) for k in range(half // tile_rows)], 0)
     row_pass((top, bottom), down, 0, plus, minus)
 
     def keep(row, col, real, imag):
@@ -252,7 +269,7 @@
     column_pass(plus, minus, across, 0, keep, keep_extra)
     total[...] = jnp.zeros_like(total)
     for r in range(spec.shape[1]):
-        turn = turns[q, r]
+        turn = turns[q, 0, r]
         flip_rows = ((turn == 1) | (turn == 2)).astype(jnp.int32)
         flip_cols = (turn >= 2).astype(jnp.int32)
         for row, col, real, imag in blocks(half):
@@ -275,50 +292,68 @@
     out[0, 0] = total[0] + total[1].T
 
 
-def pick_kernel(wanted, tiles, out, sem):
-    groups, rounds = out.shape[:2]
-    copies = [
-        pltpu.make_async_copy(tiles.at[wanted[q, i]], out.at[i, q], sem.at[q, i])
-        for i in range(groups)
-        for q in range(rounds)
-    ]
-    for copy in copies:
-        copy.start()
-    for copy in copies:
-        copy.wait()
-
-
-def spread_kernel(position, own, first, second, third, out):
-    rounds = own.shape[0]
-    groups, slots = position.shape[1], out.shape[1]
-    share = out.shape[2] // rounds
-    side = own.shape[2]
-    summed = (
-        own[...].astype(F32) + first[...].astype(F32) + second[...].astype(F32) + third[...].astype(F32)
-    )
-    span = own.shape[1] // (slots * share)
-    summed = summed.reshape(rounds, span, slots, share, side)
+def held_tile(offsets, q, i, span):
+    groups = lax.axis_size("tile")
+    step = (lax.axis_index("tile") - offsets[q, i] + groups * (groups * span)) % groups
+    held = step < span
+    return held, jnp.where(held, (offsets[q, i] + step) // groups, 0)
+
+
+def pick_kernel(offsets, tiles, out, held_tiles, in_sems, out_sems):
+    groups, rounds, tile_rows, side = out.shape
+    places = [(i, q) for i in range(groups) for q in range(rounds)]
+    held, moves = [], []
+    for i, q in places:
+        here, index = held_tile(offsets, q, i, side // tile_rows)
+        held.append(here)
+        moves.append(
+            (
+                pltpu.make_async_copy(tiles.at[index], held_tiles.at[i, q], in_sems.at[i, q]),
+                pltpu.make_async_copy(held_tiles.at[i, q], out.at[i, q], out_sems.at[i, q]),
+            )
+        )
+        pl.when(here)(moves[-1][0].start)
+    for here, (load, store) in zip(held, moves):
+
+        @pl.when(here)
+        def _():
+            load.wait()
+            store.start()
+
+    for here, (_, store) in zip(held, moves):
+        pl.when(here)(store.wait)
+
+
+def near_kernel(offsets, *refs):
+    landed, out, scratch = refs[:-2], refs[-2], refs[-1]
+    groups = out.shape[0]
+    rounds, span, far, share, side = scratch.shape
+    summed = landed[0][...].astype(F32)
+    for block in landed[1:]:
+        summed += block[...].astype(F32)
+    scratch[...] = summed.reshape(rounds, span, far, share, side)
+    own = lax.axis_index("tile")
     for i in range(groups):
         parts = []
         for q in range(rounds):
-            part = jnp.zeros((slots, share, side), F32)
-            for k in range(span):
-                part = jnp.where(position[q, i] == k, summed[q, k], part)
-            parts.append(part)
+            k = (i - offsets[q, own] + groups * (groups * span)) % groups
+            part = scratch[q, jnp.minimum(k, span - 1)]
+            parts.append(jnp.where(k < span, part, 0.0))
         out[i] = jnp.concatenate(parts, 1).astype(BF)
 
 
-def gather_kernel(wanted, holding, incoming, out):
-    rounds, groups = wanted.shape
+def gather_kernel(span, offsets, incoming, out):
+    rounds, groups = offsets.shape
     share = out.shape[1]
     out[...] = jnp.zeros_like(out)
     for i in range(groups):
-        summed = jnp.sum(incoming[i].astype(F32), 0)
+        rows = jnp.sum(incoming[i].astype(F32), 0)
         for q in range(rounds):
-
-            @pl.when(holding[q, i] == 1)
+            held, index = held_tile(offsets, q, i, span)
+
+            @pl.when(held)
             def _():
-                out[wanted[q, i]] += summed[q * share : (q + 1) * share]
+                out[index] += rows[q * share : (q + 1) * share]
 
 
 def full(shape):
@@ -328,14 +363,21 @@
 SMEM = pl.BlockSpec(memory_space=pltpu.SMEM)
 VMEM = pl.BlockSpec(memory_space=pltpu.VMEM)
 ANY = pl.BlockSpec(memory_space=pl.ANY)
-PARAMS = pltpu.CompilerParams(vmem_limit_bytes=50 * 1024 * 1024)
+SMALL = pltpu.CompilerParams(vmem_limit_bytes=12 * 1024 * 1024)
+LARGE = pltpu.CompilerParams(vmem_limit_bytes=60 * 1024 * 1024)
+
+
+def shape(dims, dtype):
+    return jax.ShapeDtypeStruct(dims, dtype)
+
+
+def per_round(dims):
+    return pl.BlockSpec((1,) + dims, lambda q: (q,) + (0,) * len(dims))
 
 
 def shards(map_tiles, sweeps, cotangents, offsets, turn_counts):
     groups = lax.axis_size("tile")
     members = lax.axis_size("sweep")
-    own_group = lax.axis_index("tile")
-    own_member = lax.axis_index("sweep")
     tile_rows, side = map_tiles.shape[1:]
     rounds = sweeps.shape[0]
     hypotheses = cotangents.shape[2]
@@ -344,55 +386,51 @@
     share = tile_rows // members
     near = 4
     far = members // near
-    turns = turn_counts[:, 0]
     sweeps = sweeps[:, 0]
     cotangents = cotangents[:, 0]
 
     order = (
         np.arange(half).reshape(span // 2, far, near, share).transpose(2, 0, 1, 3).reshape(-1)
     )
-    down, across, back, up, up_sent = make_tables(side, order)
-
-    peers = jnp.arange(groups, dtype=jnp.int32)
-    step = (own_group - offsets) % groups
-    holding = (step < span).astype(jnp.int32)
-    wanted = jnp.where(step < span, (offsets + step) // groups, 0).astype(jnp.int32)
-    own_start = lax.dynamic_slice_in_dim(offsets, own_group, 1, 1)
-    source = ((own_start + jnp.arange(span, dtype=jnp.int32)) % groups).astype(jnp.int32)
-    position = ((peers[None] - own_start) % groups).astype(jnp.int32)
+    down, across, back, up, up_sent = make_tables(side, order, near)
 
     outgoing = pl.pallas_call(
         pick_kernel,
-        out_shape=jax.ShapeDtypeStruct((groups, rounds, tile_rows, side), BF),
+        out_shape=shape((groups, rounds, tile_rows, side), BF),
         in_specs=[SMEM, ANY],
         out_specs=ANY,
-        scratch_shapes=[pltpu.SemaphoreType.DMA((rounds, groups))],
+        scratch_shapes=[
+            pltpu.VMEM((groups, rounds, tile_rows, side), BF),
+            pltpu.SemaphoreType.DMA((groups, rounds)),
+            pltpu.SemaphoreType.DMA((groups, rounds)),
+        ],
+        compiler_params=pltpu.CompilerParams(vmem_limit_bytes=60 * 1024 * 1024),
         name="pick",
-    )(wanted, map_tiles)
+    )(offsets, map_tiles)
     incoming = lax.all_to_all(outgoing, "tile", split_axis=0, concat_axis=0, tiled=True)
 
     unit = 2 * side**3
-    spec, spec_extra, sent = pl.pallas_call(
+    spec, spec_extra, *sent = pl.pallas_call(
         map_kernel,
         grid=(rounds,),
         out_shape=[
-            jax.ShapeDtypeStruct((rounds, hypotheses, side, side), BF),
-            jax.ShapeDtypeStruct((rounds, hypotheses, 2, 8, side), F32),
-            jax.ShapeDtypeStruct((rounds, near, side // near, side), BF),
+            shape((rounds, hypotheses, side, side), BF),
+            shape((rounds, hypotheses, 2, 8, side), F32),
+            *[shape((rounds, side // near, side), BF)] * near,
         ],
         in_specs=[
             SMEM,
-            pl.BlockSpec((1, side, side), lambda q: (q, 0, 0)),
-            pl.BlockSpec((1, hypotheses, side, side), lambda q: (q, 0, 0, 0)),
+            per_round((side, side)),
+            per_round((hypotheses, side, side)),
             full(down.shape),
             full(across.shape),
             full(back.shape),
             full(up_sent.shape),
         ],
         out_specs=[
-            pl.BlockSpec((1, hypotheses, side, side), lambda q: (q, 0, 0, 0)),
-            pl.BlockSpec((1, hypotheses, 2, 8, side), lambda q: (q, 0, 0, 0, 0)),
-            pl.BlockSpec((1, near, side // near, side), lambda q: (q, 0, 0, 0)),
+            per_round((hypotheses, side, side)),
+            per_round((hypotheses, 2, 8, side)),
+            *[per_round((side // near, side))] * near,
         ],
         scratch_shapes=[
             pltpu.VMEM((side, half), BF),
@@ -404,35 +442,32 @@
             pltpu.VMEM((side, side), BF),
             pltpu.VMEM((side, side), BF),
         ],
-        compiler_params=PARAMS,
+        compiler_params=LARGE,
         cost_estimate=pl.CostEstimate(
             flops=int(8 * rounds * unit), bytes_accessed=8 * 1024 * 1024, transcendentals=0
         ),
         name="map_terms",
-    )(turns, sweeps, cotangents, down, across, back, up_sent)
-
-    own_near = own_member % near
-    received = [lax.dynamic_index_in_dim(sent, own_near, 1, keepdims=False)]
+    )(turn_counts, sweeps, cotangents, down, across, back, up_sent)
+    landed = [sent[0]]
     for shift in range(1, near):
-        target = (own_near + shift) % near
-        block = lax.dynamic_index_in_dim(sent, target, 1, keepdims=False)
         pairs = [(m, m // near * near + (m + shift) % near) for m in range(members)]
-        received.append(lax.ppermute(block, "sweep", pairs))
-
-    spread = pl.pallas_call(
-        spread_kernel,
-        out_shape=jax.ShapeDtypeStruct((groups, far, rounds * share, side), BF),
+        landed.append(lax.ppermute(sent[shift], "sweep", pairs))
+
+    placed = pl.pallas_call(
+        near_kernel,
+        out_shape=shape((groups, far, rounds * share, side), BF),
         in_specs=[SMEM] + [VMEM] * near,
         out_specs=VMEM,
-        compiler_params=PARAMS,
-        name="spread",
-    )(position, *received)
+        scratch_shapes=[pltpu.VMEM((rounds, span, far, share, side), F32)],
+        compiler_params=SMALL,
+        name="near_sum",
+    )(offsets, *landed)
+    placed, incoming = lax.optimization_barrier((placed, incoming))
     index_groups = [
         [t * members + f * near + y for t in range(groups) for f in range(far)] for y in range(near)
     ]
-    spread = spread.reshape(groups * far, rounds * share, side)
-    landed = lax.all_to_all(
-        spread,
+    owned = lax.all_to_all(
+        placed.reshape(groups * far, rounds * share, side),
         ("tile", "sweep"),
         split_axis=0,
         concat_axis=0,
@@ -440,30 +475,30 @@
         axis_index_groups=index_groups,
     )
     grad_map = pl.pallas_call(
-        gather_kernel,
-        out_shape=jax.ShapeDtypeStruct((map_tiles.shape[0], share, side), F32),
-        in_specs=[SMEM, SMEM, VMEM],
+        partial(gather_kernel, span),
+        out_shape=shape((map_tiles.shape[0], share, side), F32),
+        in_specs=[SMEM, VMEM],
         out_specs=VMEM,
-        compiler_params=PARAMS,
+        compiler_params=SMALL,
         name="gather",
-    )(wanted, holding, landed.reshape(groups, far, rounds * share, side))
+    )(offsets, owned.reshape(groups, far, rounds * share, side))
 
     grad_sweeps = pl.pallas_call(
         sweep_kernel,
         grid=(rounds,),
-        out_shape=jax.ShapeDtypeStruct((rounds, 1, side, side), F32),
+        out_shape=shape((rounds, 1, side, side), F32),
         in_specs=[
             SMEM,
             SMEM,
             pl.BlockSpec((groups, 1, tile_rows, side), lambda q: (0, q, 0, 0)),
-            pl.BlockSpec((1, hypotheses, side, side), lambda q: (q, 0, 0, 0)),
-            pl.BlockSpec((1, hypotheses, 2, 8, side), lambda q: (q, 0, 0, 0, 0)),
+            per_round((hypotheses, side, side)),
+            per_round((hypotheses, 2, 8, side)),
             full(down.shape),
             full(across.shape),
             full(back.shape),
             full(up.shape),
         ],
-        out_specs=pl.BlockSpec((1, 1, side, side), lambda q: (q, 0, 0, 0)),
+        out_specs=per_round((1, side, side)),
         scratch_shapes=[
             pltpu.VMEM((side, half), BF),
             pltpu.VMEM((side, half), BF),
@@ -473,12 +508,12 @@
             pltpu.VMEM((side, side), BF),
             pltpu.VMEM((2, side, side), F32),
         ],
-        compiler_params=PARAMS,
+        compiler_params=LARGE,
         cost_estimate=pl.CostEstimate(
             flops=int(5 * rounds * unit), bytes_accessed=8 * 1024 * 1024, transcendentals=0
         ),
         name="sweep_terms",
-    )(turns, source, incoming, spec, spec_extra, down, across, back, up)
+    )(offsets, turn_counts, incoming, spec, spec_extra, down, across, back, up)
     return grad_map, grad_sweeps
 
 

time: 148 us -> 59.9 us (0.40)
  Pallas kernels: 84.2 us -> 24.2 us
  waiting for transfers between devices: 35 us -> 13.7 us
  local copies, waits for them, and re-layouts: 6.47 us -> 0.96 us
    pallas_call x5, Pallas kernels: 84.2 us -> 24.2 us  [the longest x1 9.69 us: shards(): pl.pallas_call(map_kernel, grid=(rounds,), out_shape=[shape((rounds, hypo...]
    all_to_all x1, waiting for transfers between devices: 24.9 us -> 0.01 us  [shards(): lax.all_to_all(outgoing, 'tile', split_axis=0, concat_axis=0, tiled=True)]
    unnamed x24 -> x8, local copies, waits for them, and re-layouts: 6.19 us -> 0.96 us
    all_to_all x1, waiting for transfers between devices: 0.01 us -> 2.63 us  [shards(): lax.all_to_all(placed.reshape(groups * far, rounds * share, side), ('tile...]
  transfers between devices with their start and end apart: 5 -> 5, of which waited for: 3 -> 3; matrix products, arithmetic and copies ran while one was open for 1% -> 0% of each run, Pallas kernels for 45% -> 33%
where the time goes in v1:
time: 59.9 us; the launch traced here: 59.4 us
  Pallas kernels  24.2 us (40%)
  starting transfers between devices  19.8 us (33%)
  waiting for transfers between devices  13.7 us (23%)
  local copies, waits for them, and re-layouts  0.96 us (2%)
  between operations  0.67 us (1%)
    ppermute x3, waiting for transfers between devices, shards(): landed.append(lax.ppermute(sent[shift], 'sweep', pairs))  11.1 us
    pallas_call x1, Pallas kernels, shards(): pl.pallas_call(map_kernel, grid=(rounds,), out_shape=[shape((rounds, hypo...  9.69 us
    all_to_all x1, starting transfers between devices, shards(): lax.all_to_all(placed.reshape(groups * far, rounds * share, side), ('tile...  8.97 us
    pallas_call x1, Pallas kernels, shards(): pl.pallas_call(sweep_kernel, grid=(rounds,), out_shape=shape((rounds, 1,...  8.38 us
    all_to_all x1, starting transfers between devices, shards(): lax.all_to_all(outgoing, 'tile', split_axis=0, concat_axis=0, tiled=True)  5.78 us
    ppermute x3, starting transfers between devices, shards(): landed.append(lax.ppermute(sent[shift], 'sweep', pairs))  5.08 us
    pallas_call x1, Pallas kernels, shards(): pl.pallas_call(pick_kernel, out_shape=shape((groups, rounds, tile_rows, s...  2.96 us
    all_to_all x1, waiting for transfers between devices, shards(): lax.all_to_all(placed.reshape(groups * far, rounds * share, side), ('tile...  2.63 us
  transfers between devices with their start and end apart: 5, of which 3 were waited for; matrix products, arithmetic and copies ran while one was open for 0% of the time, Pallas kernels for 33%

profile of v1, /device:TPU:1, one launch (start us, length us, event | category | flops | bytes accessed | tf_op | source)
XLA Modules:
  0.0 59.4 jit_solution(14177319866489664255)
XLA Ops:
  0.6 3.0 %pick.1 = bf16[8,2,128,512]{3,2,1,0:T(8,128)(2,1)} custom-call(s32[2,8]{1,0:T(2,128)} %offsets.7, bf16[16,128,512]{2,1,0:T(8,128)(2,1)} %tiles.1), custom_call_target="tpu_custom_call" | custom-call | tf_op jit(solution)/shard_map/pick/pallas_call | solution.py:397
  3.6 5.8 %all-to-all-start = ((bf16[8,2,128,512]{3,2,1,0:T(8,128)(2,1)}), bf16[8,2,128,512]{3,2,1,0:T(8,128)(2,1)S(1)}, u32[]{:S(2)}, u32[]{:S(2)}) async-start(bf16[8,2,128,512]{3,2,1,0:T(8,128)(2,1)} %pick.1), calls=%async_computation | async-start | bytes 4194304 | tf_op jit(solution)/shard_map/all_to_all | solution.py:410
  9.4 0.0 copy-start.1
  9.4 9.7 %map_terms.1 = (bf16[2,2,512,512]{3,2,1,0:T(8,128)(2,1)}, f32[2,2,2,8,512]{4,3,2,1,0:T(8,128)}, bf16[2,128,512]{2,1,0:T(8,128)(2,1)}, bf16[2,128,512]{2,1,0:T(8,...) custom-call(s32[2,1,2]{2,1,0:T(1,128)} %turns.3, bf16[2,512,512]{2,1,0:T(8,128)(2,1)} %bitcast.6, ...), custom_call_target="tpu_custom_call" | custom-call | flops 4294967296 | bytes 8388608 | tf_op jit(solution)/shard_map/map_terms/pallas_call | solution.py:413
  19.1 1.3 %collective-permute-start = (bf16[2,128,512]{2,1,0:T(8,128)(2,1)}, bf16[2,128,512]{2,1,0:T(8,128)(2,1)S(1)}, u32[]{:S(2)}, u32[]{:S(2)}) collective-permute-start(bf16[2,128,512]{2,1,0:T(8,128)(2,1)} %get-tuple-element.11), channel_id=1, source_target_pairs={{0,1},{1,2},{2,3},{3,0},{4,5},{5,6},{6,7},{7,4},{8,9},{9,10},{10,1... | collective-permute-start | bytes 786440 | tf_op jit(solution)/shard_map/ppermute | solution.py:454
  20.4 2.6 %collective-permute-start.1 = (bf16[2,128,512]{2,1,0:T(8,128)(2,1)}, bf16[2,128,512]{2,1,0:T(8,128)(2,1)S(1)}, u32[]{:S(2)}, u32[]{:S(2)}) collective-permute-start(bf16[2,128,512]{2,1,0:T(8,128)(2,1)} %get-tuple-element.12), channel_id=1, source_target_pairs={{0,2},{1,3},{2,0},{3,1},{4,6},{5,7},{6,4},{7,5},{8,10},{9,11},{10,... | collective-permute-start | bytes 786440 | tf_op jit(solution)/shard_map/ppermute | solution.py:454
  23.0 1.1 %collective-permute-start.2 = (bf16[2,128,512]{2,1,0:T(8,128)(2,1)}, bf16[2,128,512]{2,1,0:T(8,128)(2,1)S(1)}, u32[]{:S(2)}, u32[]{:S(2)}) collective-permute-start(bf16[2,128,512]{2,1,0:T(8,128)(2,1)} %get-tuple-element.13), channel_id=1, source_target_pairs={{0,3},{1,0},{2,1},{3,2},{4,7},{5,4},{6,5},{7,6},{8,11},{9,8},{10,9... | collective-permute-start | bytes 786440 | tf_op jit(solution)/shard_map/ppermute | solution.py:454
  24.1 4.4 %collective-permute-done.refs_1_ = bf16[2,128,512]{2,1,0:T(8,128)(2,1)S(1)} collective-permute-done((bf16[2,128,512]{2,1,0:T(8,128)(2,1)}, bf16[2,128,512]{2,1,0:T(8,128)(2,1)S(1)}, u32[]{:S(2)}, u32[]{:S(2)}) %collective-permute-start) | collective-permute-done | bytes 262176 | tf_op jit(solution)/shard_map/ppermute | solution.py:454
  28.5 6.7 %collective-permute-done.1.refs_2_ = bf16[2,128,512]{2,1,0:T(8,128)(2,1)S(1)} collective-permute-done((bf16[2,128,512]{2,1,0:T(8,128)(2,1)}, bf16[2,128,512]{2,1,0:T(8,128)(2,1)S(1)}, u32[]{:S(2)}, u32[]{:S(2)}) %collective-permute-start.1) | collective-permute-done | bytes 262176 | tf_op jit(solution)/shard_map/ppermute | solution.py:454
  35.3 0.0 collective-permute-done.2.refs_3_
  35.3 0.0 copy-done.1
  35.3 0.0 copy-start
  35.3 0.9 %copy-done = bf16[2,128,512]{2,1,0:T(8,128)(2,1)S(1)} copy-done((bf16[2,128,512]{2,1,0:T(8,128)(2,1)S(1)}, bf16[2,128,512]{2,1,0:T(8,128)(2,1)}, u32[]{:S(2)}) %copy-start) | copy-done | bytes 262168
  36.2 1.6 %near_sum.1 = bf16[8,4,16,512]{3,2,1,0:T(8,128)(2,1)} custom-call(s32[2,8]{1,0:T(2,128)S(1)} %copy-done.1, bf16[2,128,512]{2,1,0:T(8,128)(2,1)S(1)} %copy-done, bf16[2,128,512]{2,1,0:T(8,128)(2,1)S(1)} %collective-permute-done.refs_1_, bf16[2,128,512]{2,1,0:T(8,128)(2,1)S(1)} %collective-permute-done.1.refs_2_, ...), custom_call_target="tpu_custom_call" | custom-call | tf_op jit(solution)/shard_map/near_sum/pallas_call | solution.py:456
  37.8 0.0 all-to-all-done.tiles
  37.8 0.0 copy-start.3
  37.8 9.0 %all-to-all-start.1 = ((bf16[32,16,512]{2,1,0:T(8,128)(2,1)}), bf16[32,16,512]{2,1,0:T(8,128)(2,1)S(1)}, u32[]{:S(2)}, u32[]{:S(2)}) async-start(bf16[32,16,512]{2,1,0:T(8,128)(2,1)} %bitcast.2), calls=%async_computation.1 | async-start | bytes 1048576 | tf_op jit(solution)/shard_map/all_to_all | solution.py:469
  46.8 0.0 copy-done.3
  46.8 0.0 copy-start.2
  46.8 8.4 %sweep_terms.1 = f32[2,1,512,512]{3,2,1,0:T(8,128)} custom-call(s32[2,8]{1,0:T(2,128)} %offsets.7, s32[2,1,2]{2,1,0:T(1,128)} %turns.3, bf16[8,2,128,512]{3,2,1,0:T(8,128)(2,1)} %copy-done.3, bf16[2,2,512,512]{3,2,1,0:T(8,128)(2,1)} %get-tuple-element.16.spec, f32[2,2,2,8,512]{4,3,2,1,0:T(8,128)} %get-tuple-element.17.spec_extra, ...), custom_call_target="tpu_custom_call" | custom-call | flops 2684354560 | bytes 8388608 | tf_op jit(solution)/shard_map/sweep_terms/pallas_call | solution.py:486
  55.2 2.6 %all-to-all-done.1 = bf16[32,16,512]{2,1,0:T(8,128)(2,1)S(1)} async-done(((bf16[32,16,512]{2,1,0:T(8,128)(2,1)}), bf16[32,16,512]{2,1,0:T(8,128)(2,1)S(1)}, u32[]{:S(2)}, u32[]{:S(2)}) %all-to-all-start.1) | async-done | bytes 524320 | tf_op jit(solution)/shard_map/all_to_all | solution.py:469
  57.8 0.0 copy-done.2
  57.8 1.5 %gather.1 = f32[16,8,512]{2,1,0:T(8,128)} custom-call(s32[2,8]{1,0:T(2,128)S(1)} %copy-done.2, bf16[8,4,16,512]{3,2,1,0:T(8,128)(2,1)S(1)} %bitcast.4), custom_call_target="tpu_custom_call" | custom-call | tf_op jit(solution)/shard_map/gather/pallas_call | solution.py:477
Async XLA Ops:
  3.6 34.2 %all-to-all-start = ((bf16[8,2,128,512]{3,2,1,0:T(8,128)(2,1)}), bf16[8,2,128,512]{3,2,1,0:T(8,128)(2,1)S(1)}, u32[]{:S(2)}, u32[]{:S(2)}) async-start(bf16[8,2,128,512]{3,2,1,0:T(8,128)(2,1)} %pick.1), calls=%async_computation | async-start | bytes 4194304 | tf_op jit(solution)/shard_map/all_to_all | solution.py:410
  9.4 25.9 %copy-start.1 = (s32[2,8]{1,0:T(2,128)S(1)}, s32[2,8]{1,0:T(2,128)}, u32[]{:S(2)}) copy-start(s32[2,8]{1,0:T(2,128)} %offsets.7) | copy-start | bytes 196
  19.1 9.5 %collective-permute-start = (bf16[2,128,512]{2,1,0:T(8,128)(2,1)}, bf16[2,128,512]{2,1,0:T(8,128)(2,1)S(1)}, u32[]{:S(2)}, u32[]{:S(2)}) collective-permute-start(bf16[2,128,512]{2,1,0:T(8,128)(2,1)} %get-tuple-element.11), channel_id=1, source_target_pairs={{0,1},{1,2},{2,3},{3,0},{4,5},{5,6},{6,7},{7,4},{8,9},{9,10},{10,1... | collective-permute-start | bytes 786440 | tf_op jit(solution)/shard_map/ppermute | solution.py:454
  20.4 14.9 %collective-permute-start.1 = (bf16[2,128,512]{2,1,0:T(8,128)(2,1)}, bf16[2,128,512]{2,1,0:T(8,128)(2,1)S(1)}, u32[]{:S(2)}, u32[]{:S(2)}) collective-permute-start(bf16[2,128,512]{2,1,0:T(8,128)(2,1)} %get-tuple-element.12), channel_id=1, source_target_pairs={{0,2},{1,3},{2,0},{3,1},{4,6},{5,7},{6,4},{7,5},{8,10},{9,11},{10,... | collective-permute-start | bytes 786440 | tf_op jit(solution)/shard_map/ppermute | solution.py:454
  23.0 12.3 %collective-permute-start.2 = (bf16[2,128,512]{2,1,0:T(8,128)(2,1)}, bf16[2,128,512]{2,1,0:T(8,128)(2,1)S(1)}, u32[]{:S(2)}, u32[]{:S(2)}) collective-permute-start(bf16[2,128,512]{2,1,0:T(8,128)(2,1)} %get-tuple-element.13), channel_id=1, source_target_pairs={{0,3},{1,0},{2,1},{3,2},{4,7},{5,4},{6,5},{7,6},{8,11},{9,8},{10,9... | collective-permute-start | bytes 786440 | tf_op jit(solution)/shard_map/ppermute | solution.py:454
  35.3 1.0 %copy-start = (bf16[2,128,512]{2,1,0:T(8,128)(2,1)S(1)}, bf16[2,128,512]{2,1,0:T(8,128)(2,1)}, u32[]{:S(2)}) copy-start(bf16[2,128,512]{2,1,0:T(8,128)(2,1)} %get-tuple-element.10.refs_0_) | copy-start | bytes 786436
  37.8 9.0 %copy-start.3 = (bf16[8,2,128,512]{3,2,1,0:T(8,128)(2,1)}, bf16[8,2,128,512]{3,2,1,0:T(8,128)(2,1)S(1)}, u32[]{:S(2)}) copy-start(bf16[8,2,128,512]{3,2,1,0:T(8,128)(2,1)S(1)} %all-to-all-done.tiles) | copy-start | bytes 6291460
  37.8 20.0 %all-to-all-start.1 = ((bf16[32,16,512]{2,1,0:T(8,128)(2,1)}), bf16[32,16,512]{2,1,0:T(8,128)(2,1)S(1)}, u32[]{:S(2)}, u32[]{:S(2)}) async-start(bf16[32,16,512]{2,1,0:T(8,128)(2,1)} %bitcast.2), calls=%async_computation.1 | async-start | bytes 1048576 | tf_op jit(solution)/shard_map/all_to_all | solution.py:469
  46.8 11.0 %copy-start.2 = (s32[2,8]{1,0:T(2,128)S(1)}, s32[2,8]{1,0:T(2,128)}, u32[]{:S(2)}) copy-start(s32[2,8]{1,0:T(2,128)} %offsets.7) | copy-start | bytes 196

commit v2 on v1

--- a/solution.py
+++ b/solution.py
@@ -157,41 +157,55 @@
 
 
 def map_kernel(
-    turns, sweep, cots, down, across, back, up_sent, spec, spec_extra, *rest
+    offsets, turns, tiles, sweep, cots, down, across, back, up_sent,
+    outgoing, spec, spec_extra, *rest
 ):
-    q = pl.program_id(0)
     near = up_sent.shape[1]
     sent, rest = rest[:near], rest[near:]
-    plus, minus, swept, swept_extra, total, total_extra, packed, middle = rest
+    plus, minus, swept, swept_extra, total, total_extra, packed, middle = rest[:8]
+    staged, in_sems, out_sems = rest[8:]
+    q = pl.program_id(0)
+    rounds = outgoing.shape[1]
     side = sweep.shape[1]
     half = side // 2
     quarter = half // 2
+    moves = pick(offsets, tiles, outgoing, staged, in_sems, out_sems, side // tiles.shape[1])
+
+    @pl.when(q == 0)
+    def _():
+        for here, load, _ in moves:
+            pl.when(here)(load.start)
+
     hypotheses = cots.shape[1]
 
+    flips = []
     for r in range(hypotheses):
         turn = turns[q, 0, r]
         flip_rows = ((turn == 1) | (turn == 2)).astype(jnp.int32)
-        flip_cols = (turn >= 2).astype(jnp.int32)
+        flips.append((turn >= 2).astype(jnp.int32))
 
         @pl.when(turn % 2 == 0)
         def _():
-            row_pass((sweep[0, :half], sweep[0, half:]), down, flip_rows, plus, minus)
+            row_pass((sweep[0, :half], sweep[0, half:]), down, flip_rows, plus.at[r], minus.at[r])
 
         @pl.when(turn % 2 == 1)
         def _():
-            row_pass_turned(sweep.at[0], down, flip_rows, plus, minus)
+            row_pass_turned(sweep.at[0], down, flip_rows, plus.at[r], minus.at[r])
+
+    for r in range(hypotheses):
+        cot = hypotheses + r
 
         def keep(row, col, real, imag):
             rows = slice(row * quarter, (row + 1) * quarter)
-            swept[0, rows, col * half : (col + 1) * half] = real
-            swept[1, rows, col * half : (col + 1) * half] = imag
+            swept[r, 0, rows, col * half : (col + 1) * half] = real
+            swept[r, 1, rows, col * half : (col + 1) * half] = imag
 
         def keep_extra(col, real, imag):
-            swept_extra[0, :, col * half : (col + 1) * half] = real
-            swept_extra[1, :, col * half : (col + 1) * half] = imag
-
-        column_pass(plus, minus, across, flip_cols, keep, keep_extra)
-        row_pass((cots[0, r, :half], cots[0, r, half:]), down, 0, plus, minus)
+            swept_extra[r, 0, :, col * half : (col + 1) * half] = real
+            swept_extra[r, 1, :, col * half : (col + 1) * half] = imag
+
+        column_pass(plus.at[r], minus.at[r], across, flips[r], keep, keep_extra)
+        row_pass((cots[0, r, :half], cots[0, r, half:]), down, 0, plus.at[cot], minus.at[cot])
 
         def meet(row, col, real, imag):
             base = row * half
@@ -199,7 +213,7 @@
             rows = slice(row * quarter, (row + 1) * quarter)
             spec[0, r, base : base + quarter, cols] = real.astype(BF)
             spec[0, r, base + quarter : base + half, cols] = imag.astype(BF)
-            sr, si = swept[0, rows, cols], swept[1, rows, cols]
+            sr, si = swept[r, 0, rows, cols], swept[r, 1, rows, cols]
             tr, ti = real * sr - imag * si, real * si + imag * sr
             if r > 0:
                 tr, ti = total[0, rows, cols] + tr, total[1, rows, cols] + ti
@@ -216,14 +230,14 @@
             cols = slice(col * half, (col + 1) * half)
             spec_extra[0, r, 0, :, cols] = real
             spec_extra[0, r, 1, :, cols] = imag
-            sr, si = swept_extra[0, :, cols], swept_extra[1, :, cols]
+            sr, si = swept_extra[r, 0, :, cols], swept_extra[r, 1, :, cols]
             tr, ti = real * sr - imag * si, real * si + imag * sr
             if r > 0:
                 tr, ti = total_extra[0, :, cols] + tr, total_extra[1, :, cols] + ti
             total_extra[0, :, cols] = tr
             total_extra[1, :, cols] = ti
 
-        column_pass(plus, minus, across, 0, meet, meet_extra)
+        column_pass(plus.at[cot], minus.at[cot], across, 0, meet, meet_extra)
 
     _, own = members_of(near)
     ahead = [(own + shift) % near for shift in range(near)]
@@ -238,24 +252,39 @@
         sent[shift][0, :rows] = top[shift * rows : (shift + 1) * rows]
         sent[shift][0, rows:] = bottom[shift * rows : (shift + 1) * rows]
 
+    @pl.when(q == 0)
+    def _():
+        for here, load, store in moves:
+
+            @pl.when(here)
+            def _():
+                load.wait()
+                store.start()
+
+    @pl.when(q == rounds - 1)
+    def _():
+        for here, _, store in moves:
+            pl.when(here)(store.wait)
+
 
 def sweep_kernel(
-    offsets, turns, tiles, spec, spec_extra, down, across, back, up, out,
-    plus, minus, window, window_extra, packed, middle, total,
+    offsets, turns, kept, others, spec, spec_extra, down, across, back, up, out,
+    field, plus, minus, window, window_extra, packed, middle, total,
 ):
     q = pl.program_id(0)
     side = out.shape[2]
     half = side // 2
     quarter = half // 2
-    groups, _, tile_rows, _ = tiles.shape
-    start = offsets[q, lax.axis_index("tile")]
-
-    def tile(k):
-        return tiles[(start + k) % groups, 0]
-
-    top = jnp.concatenate([tile(k) for k in range(half // tile_rows)], 0)
-    bottom = jnp.concatenate([tile(k + half // tile_rows) for k in range(half // tile_rows)], 0)
-    row_pass((top, bottom), down, 0, plus, minus)
+    span, rows_kept = kept.shape[1:3]
+    parts = others.shape[0] + 1
+    own_part, _ = members_of(near=others.shape[0] + 1)
+    for shift in range(parts):
+        source = kept if shift == 0 else others.at[shift - 1]
+        part = (own_part - shift + parts) % parts
+        for k in range(span):
+            at = pl.multiple_of((parts * k + part) * rows_kept, rows_kept)
+            field[pl.ds(at, rows_kept), :] = source[0, k]
+    row_pass((field[:half], field[half:]), down, 0, plus, minus)
 
     def keep(row, col, real, imag):
         rows = slice(row * quarter, (row + 1) * quarter)
@@ -268,13 +297,13 @@
 
     column_pass(plus, minus, across, 0, keep, keep_extra)
     total[...] = jnp.zeros_like(total)
-    for r in range(spec.shape[1]):
+
+    def one_rotation(r, carry):
         turn = turns[q, 0, r]
         flip_rows = ((turn == 1) | (turn == 2)).astype(jnp.int32)
         flip_cols = (turn >= 2).astype(jnp.int32)
         for row, col, real, imag in blocks(half):
-            rows = slice(row * quarter, (row + 1) * quarter)
-            cols = real[1]
+            rows, cols = slice(row * quarter, (row + 1) * quarter), real[1]
             gr, gi = spec[(0, r) + real].astype(F32), spec[(0, r) + imag].astype(F32)
             wr, wi = window[0, rows, cols], window[1, rows, cols]
             br, bi = gr * wr + gi * wi, gr * wi - gi * wr
@@ -289,6 +318,9 @@
         )
         total[turn % 2, :half] += top
         total[turn % 2, half:] += bottom
+        return carry
+
+    lax.fori_loop(0, spec.shape[1], one_rotation, 0)
     out[0, 0] = total[0] + total[1].T
 
 
@@ -299,32 +331,33 @@
     return held, jnp.where(held, (offsets[q, i] + step) // groups, 0)
 
 
-def pick_kernel(offsets, tiles, out, held_tiles, in_sems, out_sems):
-    groups, rounds, tile_rows, side = out.shape
-    places = [(i, q) for i in range(groups) for q in range(rounds)]
-    held, moves = [], []
-    for i, q in places:
-        here, index = held_tile(offsets, q, i, side // tile_rows)
-        held.append(here)
-        moves.append(
-            (
-                pltpu.make_async_copy(tiles.at[index], held_tiles.at[i, q], in_sems.at[i, q]),
-                pltpu.make_async_copy(held_tiles.at[i, q], out.at[i, q], out_sems.at[i, q]),
+def pick(offsets, tiles, out, staged, in_sems, out_sems, span):
+    groups, rounds, rows, _ = out.shape
+    part, _ = members_of(tiles.shape[1] // rows)
+    first = pl.multiple_of(part * rows, rows)
+    moves = []
+    for i in range(groups):
+        for q in range(rounds):
+            here, index = held_tile(offsets, q, i, span)
+            load = pltpu.make_async_copy(
+                tiles.at[index, pl.ds(first, rows)], staged.at[i, q], in_sems.at[i, q]
             )
-        )
-        pl.when(here)(moves[-1][0].start)
-    for here, (load, store) in zip(held, moves):
-
-        @pl.when(here)
-        def _():
-            load.wait()
-            store.start()
-
-    for here, (_, store) in zip(held, moves):
-        pl.when(here)(store.wait)
-
-
-def near_kernel(offsets, *refs):
+            store = pltpu.make_async_copy(staged.at[i, q], out.at[i, q], out_sems.at[i, q])
+            moves.append((here, load, store))
+    return moves
+
+
+def choose_kernel(offsets, incoming, out, token):
+    rounds, span = out.shape[:2]
+    own = lax.axis_index("tile")
+    for q in range(rounds):
+        for k in range(span):
+            out[q, k] = incoming[(offsets[q, own] + k) % incoming.shape[0], q]
+    token[...] = jnp.zeros_like(token)
+
+
+def near_kernel(offsets, token, *refs):
+    del token
     landed, out, scratch = refs[:-2], refs[-2], refs[-1]
     groups = out.shape[0]
     rounds, span, far, share, side = scratch.shape
@@ -394,60 +427,68 @@
     )
     down, across, back, up, up_sent = make_tables(side, order, near)
 
-    outgoing = pl.pallas_call(
-        pick_kernel,
-        out_shape=shape((groups, rounds, tile_rows, side), BF),
-        in_specs=[SMEM, ANY],
-        out_specs=ANY,
-        scratch_shapes=[
-            pltpu.VMEM((groups, rounds, tile_rows, side), BF),
-            pltpu.SemaphoreType.DMA((groups, rounds)),
-            pltpu.SemaphoreType.DMA((groups, rounds)),
-        ],
-        compiler_params=pltpu.CompilerParams(vmem_limit_bytes=60 * 1024 * 1024),
-        name="pick",
-    )(offsets, map_tiles)
-    incoming = lax.all_to_all(outgoing, "tile", split_axis=0, concat_axis=0, tiled=True)
-
+    part_rows = tile_rows // far
     unit = 2 * side**3
-    spec, spec_extra, *sent = pl.pallas_call(
+    outgoing, spec, spec_extra, *sent = pl.pallas_call(
         map_kernel,
         grid=(rounds,),
         out_shape=[
+            shape((groups, rounds, part_rows, side), BF),
             shape((rounds, hypotheses, side, side), BF),
             shape((rounds, hypotheses, 2, 8, side), F32),
             *[shape((rounds, side // near, side), BF)] * near,
         ],
         in_specs=[
             SMEM,
+            SMEM,
+            ANY,
             per_round((side, side)),
             per_round((hypotheses, side, side)),
             full(down.shape),
             full(across.shape),
-            full(back.shape),
+            full((1,) + back.shape[1:]),
             full(up_sent.shape),
         ],
         out_specs=[
+            ANY,
             per_round((hypotheses, side, side)),
             per_round((hypotheses, 2, 8, side)),
             *[per_round((side // near, side))] * near,
         ],
         scratch_shapes=[
-            pltpu.VMEM((side, half), BF),
-            pltpu.VMEM((side, half), BF),
-            pltpu.VMEM((2, half, side), F32),
-            pltpu.VMEM((2, 8, side), F32),
+            pltpu.VMEM((2 * hypotheses, side, half), BF),
+            pltpu.VMEM((2 * hypotheses, side, half), BF),
+            pltpu.VMEM((hypotheses, 2, half, side), F32),
+            pltpu.VMEM((hypotheses, 2, 8, side), F32),
             pltpu.VMEM((2, half, side), F32),
             pltpu.VMEM((2, 8, side), F32),
             pltpu.VMEM((side, side), BF),
             pltpu.VMEM((side, side), BF),
+            pltpu.VMEM((groups, rounds, part_rows, side), BF),
+            pltpu.SemaphoreType.DMA((groups, rounds)),
+            pltpu.SemaphoreType.DMA((groups, rounds)),
         ],
         compiler_params=LARGE,
         cost_estimate=pl.CostEstimate(
             flops=int(8 * rounds * unit), bytes_accessed=8 * 1024 * 1024, transcendentals=0
         ),
         name="map_terms",
-    )(turn_counts, sweeps, cotangents, down, across, back, up_sent)
+    )(offsets, turn_counts, map_tiles, sweeps, cotangents, down, across, back, up_sent)
+    incoming = lax.all_to_all(outgoing, "tile", split_axis=0, concat_axis=0, tiled=True)
+    kept, token = pl.pallas_call(
+        choose_kernel,
+        out_shape=[shape((rounds, span, part_rows, side), BF), shape((8, 128), F32)],
+        in_specs=[SMEM, VMEM],
+        out_specs=[VMEM] * 2,
+        compiler_params=SMALL,
+        name="choose",
+    )(offsets, incoming)
+    others = jnp.stack(
+        [
+            lax.ppermute(kept, "sweep", [(m, (m + shift * near) % members) for m in range(members)])
+            for shift in range(1, far)
+        ]
+    )
     landed = [sent[0]]
     for shift in range(1, near):
         pairs = [(m, m // near * near + (m + shift) % near) for m in range(members)]
@@ -456,13 +497,12 @@
     placed = pl.pallas_call(
         near_kernel,
         out_shape=shape((groups, far, rounds * share, side), BF),
-        in_specs=[SMEM] + [VMEM] * near,
+        in_specs=[SMEM, VMEM] + [VMEM] * near,
         out_specs=VMEM,
         scratch_shapes=[pltpu.VMEM((rounds, span, far, share, side), F32)],
         compiler_params=SMALL,
         name="near_sum",
-    )(offsets, *landed)
-    placed, incoming = lax.optimization_barrier((placed, incoming))
+    )(offsets, token, *landed)
     index_groups = [
         [t * members + f * near + y for t in range(groups) for f in range(far)] for y in range(near)
     ]
@@ -490,7 +530,8 @@
         in_specs=[
             SMEM,
             SMEM,
-            pl.BlockSpec((groups, 1, tile_rows, side), lambda q: (0, q, 0, 0)),
+            per_round((span, part_rows, side)),
+            pl.BlockSpec((far - 1, 1, span, part_rows, side), lambda q: (0, q, 0, 0, 0)),
             per_round((hypotheses, side, side)),
             per_round((hypotheses, 2, 8, side)),
             full(down.shape),
@@ -500,6 +541,7 @@
         ],
         out_specs=per_round((1, side, side)),
         scratch_shapes=[
+            pltpu.VMEM((side, side), BF),
             pltpu.VMEM((side, half), BF),
             pltpu.VMEM((side, half), BF),
             pltpu.VMEM((2, half, side), F32),
@@ -513,7 +555,7 @@
             flops=int(5 * rounds * unit), bytes_accessed=8 * 1024 * 1024, transcendentals=0
         ),
         name="sweep_terms",
-    )(offsets, turn_counts, incoming, spec, spec_extra, down, across, back, up)
+    )(offsets, turn_counts, kept, others, spec, spec_extra, down, across, back, up)
     return grad_map, grad_sweeps
 
 

time: 59.9 us -> 57.1 us (0.953)
  waiting for transfers between devices: 13.7 us -> 7.63 us
  starting transfers between devices: 19.8 us -> 24.1 us
  Pallas kernels: 24.2 us -> 22.4 us
  other arithmetic: 0 us -> 0.98 us
    ppermute x3, waiting for transfers between devices: 11.1 us -> 1.62 us  [shards(): landed.append(lax.ppermute(sent[shift], 'sweep', pairs))]
    ppermute x0 -> x3, starting transfers between devices: none -> 4.53 us  [shards(): lax.ppermute(kept, 'sweep', [(m, (m + shift * near) % members) for m in r...]
    all_to_all x1, waiting for transfers between devices: 0.01 us -> 4.52 us  [shards(): lax.all_to_all(outgoing, 'tile', split_axis=0, concat_axis=0, tiled=True)]
    all_to_all x1, waiting for transfers between devices: 2.63 us -> 0.51 us  [shards(): lax.all_to_all(placed.reshape(groups * far, rounds * share, side), ('tile...]
    pallas_call x2, Pallas kernels: 12.6 us -> 10.7 us  [the longest x1 10.1 us: shards(): pl.pallas_call(map_kernel, grid=(rounds,), out_shape=[shape((groups, roun...]
    ppermute x0 -> x3, waiting for transfers between devices: none -> 0.99 us  [shards(): lax.ppermute(kept, 'sweep', [(m, (m + shift * near) % members) for m in r...]
    another operation x0 -> x1, other arithmetic: none -> 0.98 us  [shards(): jnp.stack([lax.ppermute(kept, 'sweep', [(m, (m + shift * near) % members)...]
  transfers between devices with their start and end apart: 5 -> 8, of which waited for: 3 -> 4; matrix products, arithmetic and copies ran while one was open for 0% -> 2% of each run, Pallas kernels for 33% -> 19%
where the time goes in v2:
time: 57.1 us; the launch traced here: 56.8 us
  starting transfers between devices  24.1 us (42%)
  Pallas kernels  22.4 us (39%)
  waiting for transfers between devices  7.63 us (13%)
  other arithmetic  0.98 us (2%)
  local copies, waits for them, and re-layouts  0.97 us (2%)
  between operations  0.7 us (1%)
    pallas_call x1, Pallas kernels, shards(): pl.pallas_call(map_kernel, grid=(rounds,), out_shape=[shape((groups, roun...  10.1 us
    all_to_all x1, starting transfers between devices, shards(): lax.all_to_all(placed.reshape(groups * far, rounds * share, side), ('tile...  8.84 us
    pallas_call x1, Pallas kernels, shards(): pl.pallas_call(sweep_kernel, grid=(rounds,), out_shape=shape((rounds, 1,...  8.54 us
    all_to_all x1, starting transfers between devices, shards(): lax.all_to_all(outgoing, 'tile', split_axis=0, concat_axis=0, tiled=True)  5.79 us
    ppermute x3, starting transfers between devices, shards(): landed.append(lax.ppermute(sent[shift], 'sweep', pairs))  4.96 us
    ppermute x3, starting transfers between devices, shards(): lax.ppermute(kept, 'sweep', [(m, (m + shift * near) % members) for m in r...  4.53 us
    all_to_all x1, waiting for transfers between devices, shards(): lax.all_to_all(outgoing, 'tile', split_axis=0, concat_axis=0, tiled=True)  4.52 us
    ppermute x3, waiting for transfers between devices, shards(): landed.append(lax.ppermute(sent[shift], 'sweep', pairs))  1.62 us
  transfers between devices with their start and end apart: 8, of which 4 were waited for; matrix products, arithmetic and copies ran while one was open for 2% of the time, Pallas kernels for 19%

profile of v2, /device:TPU:1, one launch (start us, length us, event | category | flops | bytes accessed | tf_op | source)
XLA Modules:
  0.0 56.8 jit_solution(11794905047063195675)
XLA Ops:
  0.6 0.0 copy-start.1
  0.6 10.1 %map_terms.1 = (bf16[8,2,32,512]{3,2,1,0:T(8,128)(2,1)}, bf16[2,2,512,512]{3,2,1,0:T(8,128)(2,1)}, f32[2,2,2,8,512]{4,3,2,1,0:T(8,128)}, bf16[2,128,512]{2,1,0:T...) custom-call(s32[2,8]{1,0:T(2,128)} %offsets.9, ...), custom_call_target="tpu_custom_call" | custom-call | flops 4294967296 | bytes 8388608 | tf_op jit(solution)/shard_map/map_terms/pallas_call | solution.py:432
  10.7 5.8 %all-to-all-start = ((bf16[8,2,32,512]{3,2,1,0:T(8,128)(2,1)}), bf16[8,2,32,512]{3,2,1,0:T(8,128)(2,1)S(1)}, u32[]{:S(2)}, u32[]{:S(2)}) async-start(bf16[8,2,32,512]{3,2,1,0:T(8,128)(2,1)} %get-tuple-element.11), calls=%async_computation | async-start | bytes 1048576 | tf_op jit(solution)/shard_map/all_to_all | solution.py:477
  16.5 1.3 %collective-permute-start = (bf16[2,128,512]{2,1,0:T(8,128)(2,1)}, bf16[2,128,512]{2,1,0:T(8,128)(2,1)S(1)}, u32[]{:S(2)}, u32[]{:S(2)}) collective-permute-start(bf16[2,128,512]{2,1,0:T(8,128)(2,1)} %get-tuple-element.14), channel_id=1, source_target_pairs={{0,1},{1,2},{2,3},{3,0},{4,5},{5,6},{6,7},{7,4},{8,9},{9,10},{10,1... | collective-permute-start | bytes 786440 | tf_op jit(solution)/shard_map/ppermute | solution.py:495
  17.8 2.6 %collective-permute-start.1 = (bf16[2,128,512]{2,1,0:T(8,128)(2,1)}, bf16[2,128,512]{2,1,0:T(8,128)(2,1)S(1)}, u32[]{:S(2)}, u32[]{:S(2)}) collective-permute-start(bf16[2,128,512]{2,1,0:T(8,128)(2,1)} %get-tuple-element.15), channel_id=1, source_target_pairs={{0,2},{1,3},{2,0},{3,1},{4,6},{5,7},{6,4},{7,5},{8,10},{9,11},{10,... | collective-permute-start | bytes 786440 | tf_op jit(solution)/shard_map/ppermute | solution.py:495
  20.5 1.0 %collective-permute-start.2 = (bf16[2,128,512]{2,1,0:T(8,128)(2,1)}, bf16[2,128,512]{2,1,0:T(8,128)(2,1)S(1)}, u32[]{:S(2)}, u32[]{:S(2)}) collective-permute-start(bf16[2,128,512]{2,1,0:T(8,128)(2,1)} %get-tuple-element.16), channel_id=1, source_target_pairs={{0,3},{1,0},{2,1},{3,2},{4,7},{5,4},{6,5},{7,6},{8,11},{9,8},{10,9... | collective-permute-start | bytes 786440 | tf_op jit(solution)/shard_map/ppermute | solution.py:495
  21.5 4.5 %all-to-all-done.incoming = bf16[8,2,32,512]{3,2,1,0:T(8,128)(2,1)S(1)} async-done(((bf16[8,2,32,512]{3,2,1,0:T(8,128)(2,1)}), bf16[8,2,32,512]{3,2,1,0:T(8,128)(2,1)S(1)}, u32[]{:S(2)}, u32[]{:S(2)}) %all-to-all-start) | async-done | bytes 524320 | tf_op jit(solution)/shard_map/all_to_all | solution.py:477
  26.0 0.0 copy-done.1
  26.0 0.6 %choose.1 = (bf16[2,4,32,512]{3,2,1,0:T(8,128)(2,1)S(1)}, f32[8,128]{1,0:T(8,128)S(1)}) custom-call(s32[2,8]{1,0:T(2,128)S(1)} %copy-done.1, bf16[8,2,32,512]{3,2,1,0:T(8,128)(2,1)S(1)} %all-to-all-done.incoming), custom_call_target="tpu_custom_call" | custom-call | tf_op jit(solution)/shard_map/choose/pallas_call | solution.py:478
  26.6 0.0 copy-start.3
  26.6 3.9 %collective-permute-start.5 = (bf16[2,4,32,512]{3,2,1,0:T(8,128)(2,1)S(1)}, bf16[2,4,32,512]{3,2,1,0:T(8,128)(2,1)S(1)}, u32[]{:S(2)}, u32[]{:S(2)}) collective-permute-start(bf16[2,4,32,512]{3,2,1,0:T(8,128)(2,1)S(1)} %get-tuple-element.17.kept), channel_id=1, source_target_pairs={{0,12},{1,13},{2,14},{3,15},{4,0},{5,1},{6,2},{7,3},{8,4},{9,5},{1... | collective-permute-start | bytes 786440 | tf_op jit(solution)/shard_map/ppermute | solution.py:488
  30.5 0.0 collective-permute-start.4
  30.5 0.0 collective-permute-done.refs_1_
  30.5 0.7 %collective-permute-start.3 = (bf16[2,4,32,512]{3,2,1,0:T(8,128)(2,1)S(1)}, bf16[2,4,32,512]{3,2,1,0:T(8,128)(2,1)S(1)}, u32[]{:S(2)}, u32[]{:S(2)}) collective-permute-start(bf16[2,4,32,512]{3,2,1,0:T(8,128)(2,1)S(1)} %get-tuple-element.17.kept), channel_id=1, source_target_pairs={{0,4},{1,5},{2,6},{3,7},{4,8},{5,9},{6,10},{7,11},{8,12},{9,13},{1... | collective-permute-start | bytes 786440 | tf_op jit(solution)/shard_map/ppermute | solution.py:488
  31.2 1.6 %collective-permute-done.1.refs_2_ = bf16[2,128,512]{2,1,0:T(8,128)(2,1)S(1)} collective-permute-done((bf16[2,128,512]{2,1,0:T(8,128)(2,1)}, bf16[2,128,512]{2,1,0:T(8,128)(2,1)S(1)}, u32[]{:S(2)}, u32[]{:S(2)}) %collective-permute-start.1) | collective-permute-done | bytes 262176 | tf_op jit(solution)/shard_map/ppermute | solution.py:495
  32.8 0.0 collective-permute-done.2.refs_3_
  32.8 0.0 copy-start
  32.8 0.9 %copy-done = bf16[2,128,512]{2,1,0:T(8,128)(2,1)S(1)} copy-done((bf16[2,128,512]{2,1,0:T(8,128)(2,1)S(1)}, bf16[2,128,512]{2,1,0:T(8,128)(2,1)}, u32[]{:S(2)}) %copy-start) | copy-done | bytes 262168
  33.7 1.6 %near_sum.1 = bf16[8,4,16,512]{3,2,1,0:T(8,128)(2,1)} custom-call(s32[2,8]{1,0:T(2,128)S(1)} %copy-done.1, f32[8,128]{1,0:T(8,128)S(1)} %get-tuple-element.12.token, bf16[2,128,512]{2,1,0:T(8,128)(2,1)S(1)} %copy-done, bf16[2,128,512]{2,1,0:T(8,128)(2,1)S(1)} %collective-permute-done.refs_1_, bf16[2,128,512]{2,1,0:T(8,128)(2,1)S(1)} %collective-permute-done.1.refs_2_, ...), custom_call_target="tpu_custom_call" | custom-call | tf_op jit(solution)/shard_map/near_sum/pallas_call | solution.py:497
  35.3 8.8 %all-to-all-start.1 = ((bf16[32,16,512]{2,1,0:T(8,128)(2,1)}), bf16[32,16,512]{2,1,0:T(8,128)(2,1)S(1)}, u32[]{:S(2)}, u32[]{:S(2)}) async-start(bf16[32,16,512]{2,1,0:T(8,128)(2,1)} %bitcast.2), calls=%async_computation.1 | async-start | bytes 1048576 | tf_op jit(solution)/shard_map/all_to_all | solution.py:509
  44.2 0.0 collective-permute-done.5
  44.2 0.0 collective-permute-done.4
  44.2 1.0 %collective-permute-done.3 = bf16[2,4,32,512]{3,2,1,0:T(8,128)(2,1)S(1)} collective-permute-done((bf16[2,4,32,512]{3,2,1,0:T(8,128)(2,1)S(1)}, bf16[2,4,32,512]{3,2,1,0:T(8,128)(2,1)S(1)}, u32[]{:S(2)}, u32[]{:S(2)}) %collective-permute-start.3) | collective-permute-done | bytes 262176 | tf_op jit(solution)/shard_map/ppermute | solution.py:488
  45.2 1.0 %pad_maximum_fusion.others = bf16[3,2,4,32,512]{4,3,2,1,0:T(8,128)(2,1)} fusion(bf16[1,2,4,32,512]{4,3,2,1,0:T(8,128)(2,1)S(1)} %bitcast.8, bf16[1,2,4,32,512]{4,3,2,1,0:T(8,128)(2,1)S(1)} %bitcast.9, bf16[1,2,4,32,512]{4,3,2,1,0:T(8,128)(2,1)S(1)} %bitcast.10), kind=kLoop, calls=%fused_computation | loop fusion | flops 786432 | bytes 1572864 | tf_op jit(solution)/shard_map/stack | solution.py:486
  46.2 0.0 copy-done.3
  46.2 0.0 copy-start.2
  46.2 8.5 %sweep_terms.1 = f32[2,1,512,512]{3,2,1,0:T(8,128)} custom-call(s32[2,8]{1,0:T(2,128)} %offsets.9, s32[2,1,2]{2,1,0:T(1,128)} %turns.3, bf16[2,4,32,512]{3,2,1,0:T(8,128)(2,1)} %copy-done.3, bf16[3,2,4,32,512]{4,3,2,1,0:T(8,128)(2,1)} %pad_maximum_fusion.others, bf16[2,2,512,512]{3,2,1,0:T(8,128)(2,1)} %get-tuple-element.18.spec, ...), custom_call_target="tpu_custom_call" | custom-call | flops 2684354560 | bytes 8388608 | tf_op jit(solution)/shard_map/sweep_terms/pallas_call | solution.py:526
  54.7 0.5 all-to-all-done.1
  55.2 0.0 copy-done.2
  55.2 1.5 %gather.1 = f32[16,8,512]{2,1,0:T(8,128)} custom-call(s32[2,8]{1,0:T(2,128)S(1)} %copy-done.2, bf16[8,4,16,512]{3,2,1,0:T(8,128)(2,1)S(1)} %bitcast.7), custom_call_target="tpu_custom_call" | custom-call | tf_op jit(solution)/shard_map/gather/pallas_call | solution.py:517
Async XLA Ops:
  0.6 25.4 %copy-start.1 = (s32[2,8]{1,0:T(2,128)S(1)}, s32[2,8]{1,0:T(2,128)}, u32[]{:S(2)}) copy-start(s32[2,8]{1,0:T(2,128)} %offsets.9) | copy-start | bytes 196
  10.7 15.3 %all-to-all-start = ((bf16[8,2,32,512]{3,2,1,0:T(8,128)(2,1)}), bf16[8,2,32,512]{3,2,1,0:T(8,128)(2,1)S(1)}, u32[]{:S(2)}, u32[]{:S(2)}) async-start(bf16[8,2,32,512]{3,2,1,0:T(8,128)(2,1)} %get-tuple-element.11), calls=%async_computation | async-start | bytes 1048576 | tf_op jit(solution)/shard_map/all_to_all | solution.py:477
  16.5 13.9 %collective-permute-start = (bf16[2,128,512]{2,1,0:T(8,128)(2,1)}, bf16[2,128,512]{2,1,0:T(8,128)(2,1)S(1)}, u32[]{:S(2)}, u32[]{:S(2)}) collective-permute-start(bf16[2,128,512]{2,1,0:T(8,128)(2,1)} %get-tuple-element.14), channel_id=1, source_target_pairs={{0,1},{1,2},{2,3},{3,0},{4,5},{5,6},{6,7},{7,4},{8,9},{9,10},{10,1... | collective-permute-start | bytes 786440 | tf_op jit(solution)/shard_map/ppermute | solution.py:495
  17.8 14.9 %collective-permute-start.1 = (bf16[2,128,512]{2,1,0:T(8,128)(2,1)}, bf16[2,128,512]{2,1,0:T(8,128)(2,1)S(1)}, u32[]{:S(2)}, u32[]{:S(2)}) collective-permute-start(bf16[2,128,512]{2,1,0:T(8,128)(2,1)} %get-tuple-element.15), channel_id=1, source_target_pairs={{0,2},{1,3},{2,0},{3,1},{4,6},{5,7},{6,4},{7,5},{8,10},{9,11},{10,... | collective-permute-start | bytes 786440 | tf_op jit(solution)/shard_map/ppermute | solution.py:495
  20.5 12.3 %collective-permute-start.2 = (bf16[2,128,512]{2,1,0:T(8,128)(2,1)}, bf16[2,128,512]{2,1,0:T(8,128)(2,1)S(1)}, u32[]{:S(2)}, u32[]{:S(2)}) collective-permute-start(bf16[2,128,512]{2,1,0:T(8,128)(2,1)} %get-tuple-element.16), channel_id=1, source_target_pairs={{0,3},{1,0},{2,1},{3,2},{4,7},{5,4},{6,5},{7,6},{8,11},{9,8},{10,9... | collective-permute-start | bytes 786440 | tf_op jit(solution)/shard_map/ppermute | solution.py:495
  26.6 19.6 %copy-start.3 = (bf16[2,4,32,512]{3,2,1,0:T(8,128)(2,1)}, bf16[2,4,32,512]{3,2,1,0:T(8,128)(2,1)S(1)}, u32[]{:S(2)}) copy-start(bf16[2,4,32,512]{3,2,1,0:T(8,128)(2,1)S(1)} %get-tuple-element.17.kept) | copy-start | bytes 786436
  26.6 17.6 %collective-permute-start.5 = (bf16[2,4,32,512]{3,2,1,0:T(8,128)(2,1)S(1)}, bf16[2,4,32,512]{3,2,1,0:T(8,128)(2,1)S(1)}, u32[]{:S(2)}, u32[]{:S(2)}) collective-permute-start(bf16[2,4,32,512]{3,2,1,0:T(8,128)(2,1)S(1)} %get-tuple-element.17.kept), channel_id=1, source_target_pairs={{0,12},{1,13},{2,14},{3,15},{4,0},{5,1},{6,2},{7,3},{8,4},{9,5},{1... | collective-permute-start | bytes 786440 | tf_op jit(solution)/shard_map/ppermute | solution.py:488
  30.5 13.7 %collective-permute-start.4 = (bf16[2,4,32,512]{3,2,1,0:T(8,128)(2,1)S(1)}, bf16[2,4,32,512]{3,2,1,0:T(8,128)(2,1)S(1)}, u32[]{:S(2)}, u32[]{:S(2)}) collective-permute-start(bf16[2,4,32,512]{3,2,1,0:T(8,128)(2,1)S(1)} %get-tuple-element.17.kept), channel_id=1, source_target_pairs={{0,8},{1,9},{2,10},{3,11},{4,12},{5,13},{6,14},{7,15},{8,0},{9,1},... | collective-permute-start | bytes 786440 | tf_op jit(solution)/shard_map/ppermute | solution.py:488
  30.5 14.7 %collective-permute-start.3 = (bf16[2,4,32,512]{3,2,1,0:T(8,128)(2,1)S(1)}, bf16[2,4,32,512]{3,2,1,0:T(8,128)(2,1)S(1)}, u32[]{:S(2)}, u32[]{:S(2)}) collective-permute-start(bf16[2,4,32,512]{3,2,1,0:T(8,128)(2,1)S(1)} %get-tuple-element.17.kept), channel_id=1, source_target_pairs={{0,4},{1,5},{2,6},{3,7},{4,8},{5,9},{6,10},{7,11},{8,12},{9,13},{1... | collective-permute-start | bytes 786440 | tf_op jit(solution)/shard_map/ppermute | solution.py:488
  32.8 1.0 %copy-start = (bf16[2,128,512]{2,1,0:T(8,128)(2,1)S(1)}, bf16[2,128,512]{2,1,0:T(8,128)(2,1)}, u32[]{:S(2)}) copy-start(bf16[2,128,512]{2,1,0:T(8,128)(2,1)} %get-tuple-element.13.refs_0_) | copy-start | bytes 786436
  35.3 19.9 %all-to-all-start.1 = ((bf16[32,16,512]{2,1,0:T(8,128)(2,1)}), bf16[32,16,512]{2,1,0:T(8,128)(2,1)S(1)}, u32[]{:S(2)}, u32[]{:S(2)}) async-start(bf16[32,16,512]{2,1,0:T(8,128)(2,1)} %bitcast.2), calls=%async_computation.1 | async-start | bytes 1048576 | tf_op jit(solution)/shard_map/all_to_all | solution.py:509
  46.2 9.0 %copy-start.2 = (s32[2,8]{1,0:T(2,128)S(1)}, s32[2,8]{1,0:T(2,128)}, u32[]{:S(2)}) copy-start(s32[2,8]{1,0:T(2,128)} %offsets.9) | copy-start | bytes 196

commit v3 on v2

--- a/solution.py
+++ b/solution.py
@@ -267,23 +267,21 @@
             pl.when(here)(store.wait)
 
 
-def sweep_kernel(
-    offsets, turns, kept, others, spec, spec_extra, down, across, back, up, out,
-    field, plus, minus, window, window_extra, packed, middle, total,
-):
+def sweep_kernel(parts, offsets, turns, *refs):
+    quarters, refs = refs[:parts], refs[parts:]
+    spec, spec_extra, down, across, back, up, out = refs[:7]
+    field, plus, minus, window, window_extra, packed, middle, total = refs[7:]
     q = pl.program_id(0)
     side = out.shape[2]
     half = side // 2
     quarter = half // 2
-    span, rows_kept = kept.shape[1:3]
-    parts = others.shape[0] + 1
-    own_part, _ = members_of(near=others.shape[0] + 1)
+    span, rows_kept = quarters[0].shape[1:3]
+    own_part, _ = members_of(parts)
     for shift in range(parts):
-        source = kept if shift == 0 else others.at[shift - 1]
         part = (own_part - shift + parts) % parts
         for k in range(span):
             at = pl.multiple_of((parts * k + part) * rows_kept, rows_kept)
-            field[pl.ds(at, rows_kept), :] = source[0, k]
+            field[pl.ds(at, rows_kept), :] = quarters[shift][0, k]
     row_pass((field[:half], field[half:]), down, 0, plus, minus)
 
     def keep(row, col, real, imag):
@@ -298,7 +296,7 @@
     column_pass(plus, minus, across, 0, keep, keep_extra)
     total[...] = jnp.zeros_like(total)
 
-    def one_rotation(r, carry):
+    for r in range(spec.shape[1]):
         turn = turns[q, 0, r]
         flip_rows = ((turn == 1) | (turn == 2)).astype(jnp.int32)
         flip_cols = (turn >= 2).astype(jnp.int32)
@@ -311,16 +309,13 @@
                 gr, gi = spec_extra[0, r, 0, :, cols], spec_extra[0, r, 1, :, cols]
                 wr, wi = window_extra[0, :, cols], window_extra[1, :, cols]
                 br, bi = merge_row(br, bi, gr * wr + gi * wi, gr * wi - gi * wr)
-            packed[real] = br.astype(BF)
-            packed[imag] = bi.astype(BF)
+            packed[(r,) + real] = br.astype(BF)
+            packed[(r,) + imag] = bi.astype(BF)
         top, bottom = inverse(
-            packed, back, flip_cols, up, lambda u, parity: u[flip_rows, parity], middle
+            packed.at[r], back, flip_cols, up, lambda u, parity: u[flip_rows, parity], middle.at[r]
         )
         total[turn % 2, :half] += top
         total[turn % 2, half:] += bottom
-        return carry
-
-    lax.fori_loop(0, spec.shape[1], one_rotation, 0)
     out[0, 0] = total[0] + total[1].T
 
 
@@ -383,10 +378,7 @@
         rows = jnp.sum(incoming[i].astype(F32), 0)
         for q in range(rounds):
             held, index = held_tile(offsets, q, i, span)
-
-            @pl.when(held)
-            def _():
-                out[index] += rows[q * share : (q + 1) * share]
+            out[index] += jnp.where(held, rows[q * share : (q + 1) * share], 0.0)
 
 
 def full(shape):
@@ -483,12 +475,10 @@
         compiler_params=SMALL,
         name="choose",
     )(offsets, incoming)
-    others = jnp.stack(
-        [
-            lax.ppermute(kept, "sweep", [(m, (m + shift * near) % members) for m in range(members)])
-            for shift in range(1, far)
-        ]
-    )
+    quarters = [kept] + [
+        lax.ppermute(kept, "sweep", [(m, (m + shift * near) % members) for m in range(members)])
+        for shift in range(1, far)
+    ]
     landed = [sent[0]]
     for shift in range(1, near):
         pairs = [(m, m // near * near + (m + shift) % near) for m in range(members)]
@@ -524,18 +514,17 @@
     )(offsets, owned.reshape(groups, far, rounds * share, side))
 
     grad_sweeps = pl.pallas_call(
-        sweep_kernel,
+        partial(sweep_kernel, far),
         grid=(rounds,),
         out_shape=shape((rounds, 1, side, side), F32),
         in_specs=[
             SMEM,
             SMEM,
-            per_round((span, part_rows, side)),
-            pl.BlockSpec((far - 1, 1, span, part_rows, side), lambda q: (0, q, 0, 0, 0)),
+            *[per_round((span, part_rows, side))] * far,
             per_round((hypotheses, side, side)),
             per_round((hypotheses, 2, 8, side)),
-            full(down.shape),
-            full(across.shape),
+            full((1,) + down.shape[1:]),
+            full((1,) + across.shape[1:]),
             full(back.shape),
             full(up.shape),
         ],
@@ -546,8 +535,8 @@
             pltpu.VMEM((side, half), BF),
             pltpu.VMEM((2, half, side), F32),
             pltpu.VMEM((2, 8, side), F32),
-            pltpu.VMEM((side, side), BF),
-            pltpu.VMEM((side, side), BF),
+            pltpu.VMEM((hypotheses, side, side), BF),
+            pltpu.VMEM((hypotheses, side, side), BF),
             pltpu.VMEM((2, side, side), F32),
         ],
         compiler_params=LARGE,
@@ -555,7 +544,7 @@
             flops=int(5 * rounds * unit), bytes_accessed=8 * 1024 * 1024, transcendentals=0
         ),
         name="sweep_terms",
-    )(offsets, turn_counts, kept, others, spec, spec_extra, down, across, back, up)
+    )(offsets, turn_counts, *quarters, spec, spec_extra, down, across, back, up)
     return grad_map, grad_sweeps
 
 

time: 57.1 us -> 57 us (level)
  starting transfers between devices: 24.1 us -> 25.4 us
  other arithmetic: 0.98 us -> 0 us
  waiting for transfers between devices: 7.63 us -> 6.77 us
  local copies, waits for them, and re-layouts: 0.97 us -> 1.8 us
    all_to_all x1, waiting for transfers between devices: 0.51 us -> 1.9 us  [shards(): lax.all_to_all(placed.reshape(groups * far, rounds * share, side), ('tile...]
    ppermute x3, starting transfers between devices: 4.53 us -> 5.79 us  [shards(): lax.ppermute(kept, 'sweep', [(m, (m + shift * near) % members) for m in r...]
    ppermute x3, waiting for transfers between devices: 1.62 us -> 0.39 us  [shards(): landed.append(lax.ppermute(sent[shift], 'sweep', pairs))]
    another operation x1 -> x0, other arithmetic: 0.98 us -> none  [shards(): jnp.stack([lax.ppermute(kept, 'sweep', [(m, (m + shift * near) % members)...]
    ppermute x3, waiting for transfers between devices: 0.99 us -> 0.01 us  [shards(): lax.ppermute(kept, 'sweep', [(m, (m + shift * near) % members) for m in r...]
    unnamed x8 -> x14, local copies, waits for them, and re-layouts: 0.97 us -> 1.8 us
  transfers between devices with their start and end apart: 8 -> 8, of which waited for: 4 -> 3; matrix products, arithmetic and copies ran while one was open for 2% -> 0% of each run, Pallas kernels for 19% -> 18%
where the time goes in v3:
time: 57 us; the launch traced here: 56.7 us
  starting transfers between devices  25.4 us (45%)
  Pallas kernels  21.9 us (38%)
  waiting for transfers between devices  6.77 us (12%)
  local copies, waits for them, and re-layouts  1.8 us (3%)
  between operations  0.74 us (1%)
    pallas_call x1, Pallas kernels, shards(): pl.pallas_call(map_kernel, grid=(rounds,), out_shape=[shape((groups, roun...  10.1 us
    all_to_all x1, starting transfers between devices, shards(): lax.all_to_all(placed.reshape(groups * far, rounds * share, side), ('tile...  8.88 us
    pallas_call x1, Pallas kernels, shards(): pl.pallas_call(partial(sweep_kernel, far), grid=(rounds,), out_shape=shap...  8.23 us
    ppermute x3, starting transfers between devices, shards(): lax.ppermute(kept, 'sweep', [(m, (m + shift * near) % members) for m in r...  5.79 us
    all_to_all x1, starting transfers between devices, shards(): lax.all_to_all(outgoing, 'tile', split_axis=0, concat_axis=0, tiled=True)  5.73 us
    ppermute x3, starting transfers between devices, shards(): landed.append(lax.ppermute(sent[shift], 'sweep', pairs))  5.01 us
    all_to_all x1, waiting for transfers between devices, shards(): lax.all_to_all(outgoing, 'tile', split_axis=0, concat_axis=0, tiled=True)  4.47 us
    all_to_all x1, waiting for transfers between devices, shards(): lax.all_to_all(placed.reshape(groups * far, rounds * share, side), ('tile...  1.9 us
  transfers between devices with their start and end apart: 8, of which 3 were waited for; matrix products, arithmetic and copies ran while one was open for 0% of the time, Pallas kernels for 18%

profile of v3, /device:TPU:1, one launch (start us, length us, event | category | flops | bytes accessed | tf_op | source)
XLA Modules:
  0.0 56.7 jit_solution(10214713881443664165)
XLA Ops:
  0.6 0.0 copy-start.1
  0.6 10.1 %map_terms.1 = (bf16[8,2,32,512]{3,2,1,0:T(8,128)(2,1)}, bf16[2,2,512,512]{3,2,1,0:T(8,128)(2,1)}, f32[2,2,2,8,512]{4,3,2,1,0:T(8,128)}, bf16[2,128,512]{2,1,0:T...) custom-call(s32[2,8]{1,0:T(2,128)} %offsets.9, ...), custom_call_target="tpu_custom_call" | custom-call | flops 4294967296 | bytes 8388608 | tf_op jit(solution)/shard_map/map_terms/pallas_call | solution.py:424
  10.8 5.7 %all-to-all-start = ((bf16[8,2,32,512]{3,2,1,0:T(8,128)(2,1)}), bf16[8,2,32,512]{3,2,1,0:T(8,128)(2,1)S(1)}, u32[]{:S(2)}, u32[]{:S(2)}) async-start(bf16[8,2,32,512]{3,2,1,0:T(8,128)(2,1)} %get-tuple-element.11), calls=%async_computation | async-start | bytes 1048576 | tf_op jit(solution)/shard_map/all_to_all | solution.py:469
  16.5 1.3 %collective-permute-start = (bf16[2,128,512]{2,1,0:T(8,128)(2,1)}, bf16[2,128,512]{2,1,0:T(8,128)(2,1)S(1)}, u32[]{:S(2)}, u32[]{:S(2)}) collective-permute-start(bf16[2,128,512]{2,1,0:T(8,128)(2,1)} %get-tuple-element.14), channel_id=1, source_target_pairs={{0,1},{1,2},{2,3},{3,0},{4,5},{5,6},{6,7},{7,4},{8,9},{9,10},{10,1... | collective-permute-start | bytes 786440 | tf_op jit(solution)/shard_map/ppermute | solution.py:485
  17.8 2.6 %collective-permute-start.1 = (bf16[2,128,512]{2,1,0:T(8,128)(2,1)}, bf16[2,128,512]{2,1,0:T(8,128)(2,1)S(1)}, u32[]{:S(2)}, u32[]{:S(2)}) collective-permute-start(bf16[2,128,512]{2,1,0:T(8,128)(2,1)} %get-tuple-element.15), channel_id=1, source_target_pairs={{0,2},{1,3},{2,0},{3,1},{4,6},{5,7},{6,4},{7,5},{8,10},{9,11},{10,... | collective-permute-start | bytes 786440 | tf_op jit(solution)/shard_map/ppermute | solution.py:485
  20.4 1.0 %collective-permute-start.2 = (bf16[2,128,512]{2,1,0:T(8,128)(2,1)}, bf16[2,128,512]{2,1,0:T(8,128)(2,1)S(1)}, u32[]{:S(2)}, u32[]{:S(2)}) collective-permute-start(bf16[2,128,512]{2,1,0:T(8,128)(2,1)} %get-tuple-element.16), channel_id=1, source_target_pairs={{0,3},{1,0},{2,1},{3,2},{4,7},{5,4},{6,5},{7,6},{8,11},{9,8},{10,9... | collective-permute-start | bytes 786440 | tf_op jit(solution)/shard_map/ppermute | solution.py:485
  21.5 4.5 %all-to-all-done.incoming = bf16[8,2,32,512]{3,2,1,0:T(8,128)(2,1)S(1)} async-done(((bf16[8,2,32,512]{3,2,1,0:T(8,128)(2,1)}), bf16[8,2,32,512]{3,2,1,0:T(8,128)(2,1)S(1)}, u32[]{:S(2)}, u32[]{:S(2)}) %all-to-all-start) | async-done | bytes 524320 | tf_op jit(solution)/shard_map/all_to_all | solution.py:469
  26.0 0.0 copy-done.1
  26.0 0.6 %choose.1 = (bf16[2,4,32,512]{3,2,1,0:T(8,128)(2,1)S(1)}, f32[8,128]{1,0:T(8,128)S(1)}) custom-call(s32[2,8]{1,0:T(2,128)S(1)} %copy-done.1, bf16[8,2,32,512]{3,2,1,0:T(8,128)(2,1)S(1)} %all-to-all-done.incoming), custom_call_target="tpu_custom_call" | custom-call | tf_op jit(solution)/shard_map/choose/pallas_call | solution.py:470
  26.6 0.0 copy-start.3
  26.6 1.8 %collective-permute-start.3 = (bf16[2,4,32,512]{3,2,1,0:T(8,128)(2,1)S(1)}, bf16[2,4,32,512]{3,2,1,0:T(8,128)(2,1)S(1)}, u32[]{:S(2)}, u32[]{:S(2)}) collective-permute-start(bf16[2,4,32,512]{3,2,1,0:T(8,128)(2,1)S(1)} %get-tuple-element.17.refs_0_), channel_id=1, source_target_pairs={{0,4},{1,5},{2,6},{3,7},{4,8},{5,9},{6,10},{7,11},{8,12},{9,13},{1... | collective-permute-start | bytes 786440 | tf_op jit(solution)/shard_map/ppermute | solution.py:479
  28.3 3.3 %collective-permute-start.4 = (bf16[2,4,32,512]{3,2,1,0:T(8,128)(2,1)S(1)}, bf16[2,4,32,512]{3,2,1,0:T(8,128)(2,1)S(1)}, u32[]{:S(2)}, u32[]{:S(2)}) collective-permute-start(bf16[2,4,32,512]{3,2,1,0:T(8,128)(2,1)S(1)} %get-tuple-element.17.refs_0_), channel_id=1, source_target_pairs={{0,8},{1,9},{2,10},{3,11},{4,12},{5,13},{6,14},{7,15},{8,0},{9,1},... | collective-permute-start | bytes 786440 | tf_op jit(solution)/shard_map/ppermute | solution.py:479
  31.6 0.0 collective-permute-done.refs_1_
  31.6 0.7 %collective-permute-start.5 = (bf16[2,4,32,512]{3,2,1,0:T(8,128)(2,1)S(1)}, bf16[2,4,32,512]{3,2,1,0:T(8,128)(2,1)S(1)}, u32[]{:S(2)}, u32[]{:S(2)}) collective-permute-start(bf16[2,4,32,512]{3,2,1,0:T(8,128)(2,1)S(1)} %get-tuple-element.17.refs_0_), channel_id=1, source_target_pairs={{0,12},{1,13},{2,14},{3,15},{4,0},{5,1},{6,2},{7,3},{8,4},{9,5},{1... | collective-permute-start | bytes 786440 | tf_op jit(solution)/shard_map/ppermute | solution.py:479
  32.4 0.4 collective-permute-done.1.refs_2_
  32.7 0.0 collective-permute-done.2.refs_3_
  32.8 0.0 copy-start
  32.8 0.9 %copy-done = bf16[2,128,512]{2,1,0:T(8,128)(2,1)S(1)} copy-done((bf16[2,128,512]{2,1,0:T(8,128)(2,1)S(1)}, bf16[2,128,512]{2,1,0:T(8,128)(2,1)}, u32[]{:S(2)}) %copy-start) | copy-done | bytes 262168
  33.7 1.6 %near_sum.1 = bf16[8,4,16,512]{3,2,1,0:T(8,128)(2,1)} custom-call(s32[2,8]{1,0:T(2,128)S(1)} %copy-done.1, f32[8,128]{1,0:T(8,128)S(1)} %get-tuple-element.12.token, bf16[2,128,512]{2,1,0:T(8,128)(2,1)S(1)} %copy-done, bf16[2,128,512]{2,1,0:T(8,128)(2,1)S(1)} %collective-permute-done.refs_1_, bf16[2,128,512]{2,1,0:T(8,128)(2,1)S(1)} %collective-permute-done.1.refs_2_, ...), custom_call_target="tpu_custom_call" | custom-call | tf_op jit(solution)/shard_map/near_sum/pallas_call | solution.py:487
  35.3 8.9 %all-to-all-start.1 = ((bf16[32,16,512]{2,1,0:T(8,128)(2,1)}), bf16[32,16,512]{2,1,0:T(8,128)(2,1)S(1)}, u32[]{:S(2)}, u32[]{:S(2)}) async-start(bf16[32,16,512]{2,1,0:T(8,128)(2,1)} %bitcast.2), calls=%async_computation.1 | async-start | bytes 1048576 | tf_op jit(solution)/shard_map/all_to_all | solution.py:499
  44.2 0.0 collective-permute-done.3.refs_1_
  44.2 0.0 copy-start.4
  44.2 0.0 collective-permute-done.4.refs_2_
  44.2 0.0 copy-start.5
  44.2 0.0 collective-permute-done.5.refs_3_
  44.3 0.0 copy-start.6
  44.3 0.0 copy-done.3
  44.3 0.6 %copy-done.4 = bf16[2,4,32,512]{3,2,1,0:T(8,128)(2,1)} copy-done((bf16[2,4,32,512]{3,2,1,0:T(8,128)(2,1)}, bf16[2,4,32,512]{3,2,1,0:T(8,128)(2,1)S(1)}, u32[]{:S(2)}) %copy-start.4) | copy-done | bytes 262168
  44.9 0.1 copy-done.5
  45.0 0.1 copy-done.6
  45.1 0.0 copy-start.2
  45.1 8.2 %sweep_terms.1 = f32[2,1,512,512]{3,2,1,0:T(8,128)} custom-call(s32[2,8]{1,0:T(2,128)} %offsets.9, s32[2,1,2]{2,1,0:T(1,128)} %turns.3, bf16[2,4,32,512]{3,2,1,0:T(8,128)(2,1)} %copy-done.3, bf16[2,4,32,512]{3,2,1,0:T(8,128)(2,1)} %copy-done.4, bf16[2,4,32,512]{3,2,1,0:T(8,128)(2,1)} %copy-done.5, bf16[2,4,32,512]{3,2,1,0:T(8,128)(2,1)} %copy-done.6, ...), custom_call_target="tpu_custom_call" | custom-call | flops 2684354560 | bytes 8388608 | tf_op jit(solution)/shard_map/sweep_terms/pallas_call | solution.py:516
  53.3 1.9 %all-to-all-done.1 = bf16[32,16,512]{2,1,0:T(8,128)(2,1)S(1)} async-done(((bf16[32,16,512]{2,1,0:T(8,128)(2,1)}), bf16[32,16,512]{2,1,0:T(8,128)(2,1)S(1)}, u32[]{:S(2)}, u32[]{:S(2)}) %all-to-all-start.1) | async-done | bytes 524320 | tf_op jit(solution)/shard_map/all_to_all | solution.py:499
  55.2 0.0 copy-done.2
  55.2 1.4 %gather.1 = f32[16,8,512]{2,1,0:T(8,128)} custom-call(s32[2,8]{1,0:T(2,128)S(1)} %copy-done.2, bf16[8,4,16,512]{3,2,1,0:T(8,128)(2,1)S(1)} %bitcast.4), custom_call_target="tpu_custom_call" | custom-call | tf_op jit(solution)/shard_map/gather/pallas_call | solution.py:507
Async XLA Ops:
  0.6 25.3 %copy-start.1 = (s32[2,8]{1,0:T(2,128)S(1)}, s32[2,8]{1,0:T(2,128)}, u32[]{:S(2)}) copy-start(s32[2,8]{1,0:T(2,128)} %offsets.9) | copy-start | bytes 196
  10.8 15.2 %all-to-all-start = ((bf16[8,2,32,512]{3,2,1,0:T(8,128)(2,1)}), bf16[8,2,32,512]{3,2,1,0:T(8,128)(2,1)S(1)}, u32[]{:S(2)}, u32[]{:S(2)}) async-start(bf16[8,2,32,512]{3,2,1,0:T(8,128)(2,1)} %get-tuple-element.11), calls=%async_computation | async-start | bytes 1048576 | tf_op jit(solution)/shard_map/all_to_all | solution.py:469
  16.5 15.1 %collective-permute-start = (bf16[2,128,512]{2,1,0:T(8,128)(2,1)}, bf16[2,128,512]{2,1,0:T(8,128)(2,1)S(1)}, u32[]{:S(2)}, u32[]{:S(2)}) collective-permute-start(bf16[2,128,512]{2,1,0:T(8,128)(2,1)} %get-tuple-element.14), channel_id=1, source_target_pairs={{0,1},{1,2},{2,3},{3,0},{4,5},{5,6},{6,7},{7,4},{8,9},{9,10},{10,1... | collective-permute-start | bytes 786440 | tf_op jit(solution)/shard_map/ppermute | solution.py:485
  17.8 14.9 %collective-permute-start.1 = (bf16[2,128,512]{2,1,0:T(8,128)(2,1)}, bf16[2,128,512]{2,1,0:T(8,128)(2,1)S(1)}, u32[]{:S(2)}, u32[]{:S(2)}) collective-permute-start(bf16[2,128,512]{2,1,0:T(8,128)(2,1)} %get-tuple-element.15), channel_id=1, source_target_pairs={{0,2},{1,3},{2,0},{3,1},{4,6},{5,7},{6,4},{7,5},{8,10},{9,11},{10,... | collective-permute-start | bytes 786440 | tf_op jit(solution)/shard_map/ppermute | solution.py:485
  20.4 12.3 %collective-permute-start.2 = (bf16[2,128,512]{2,1,0:T(8,128)(2,1)}, bf16[2,128,512]{2,1,0:T(8,128)(2,1)S(1)}, u32[]{:S(2)}, u32[]{:S(2)}) collective-permute-start(bf16[2,128,512]{2,1,0:T(8,128)(2,1)} %get-tuple-element.16), channel_id=1, source_target_pairs={{0,3},{1,0},{2,1},{3,2},{4,7},{5,4},{6,5},{7,6},{8,11},{9,8},{10,9... | collective-permute-start | bytes 786440 | tf_op jit(solution)/shard_map/ppermute | solution.py:485
  26.6 17.7 %copy-start.3 = (bf16[2,4,32,512]{3,2,1,0:T(8,128)(2,1)}, bf16[2,4,32,512]{3,2,1,0:T(8,128)(2,1)S(1)}, u32[]{:S(2)}) copy-start(bf16[2,4,32,512]{3,2,1,0:T(8,128)(2,1)S(1)} %get-tuple-element.17.refs_0_) | copy-start | bytes 786436
  26.6 17.6 %collective-permute-start.3 = (bf16[2,4,32,512]{3,2,1,0:T(8,128)(2,1)S(1)}, bf16[2,4,32,512]{3,2,1,0:T(8,128)(2,1)S(1)}, u32[]{:S(2)}, u32[]{:S(2)}) collective-permute-start(bf16[2,4,32,512]{3,2,1,0:T(8,128)(2,1)S(1)} %get-tuple-element.17.refs_0_), channel_id=1, source_target_pairs={{0,4},{1,5},{2,6},{3,7},{4,8},{5,9},{6,10},{7,11},{8,12},{9,13},{1... | collective-permute-start | bytes 786440 | tf_op jit(solution)/shard_map/ppermute | solution.py:479
  28.3 15.9 %collective-permute-start.4 = (bf16[2,4,32,512]{3,2,1,0:T(8,128)(2,1)S(1)}, bf16[2,4,32,512]{3,2,1,0:T(8,128)(2,1)S(1)}, u32[]{:S(2)}, u32[]{:S(2)}) collective-permute-start(bf16[2,4,32,512]{3,2,1,0:T(8,128)(2,1)S(1)} %get-tuple-element.17.refs_0_), channel_id=1, source_target_pairs={{0,8},{1,9},{2,10},{3,11},{4,12},{5,13},{6,14},{7,15},{8,0},{9,1},... | collective-permute-start | bytes 786440 | tf_op jit(solution)/shard_map/ppermute | solution.py:479
  31.6 12.6 %collective-permute-start.5 = (bf16[2,4,32,512]{3,2,1,0:T(8,128)(2,1)S(1)}, bf16[2,4,32,512]{3,2,1,0:T(8,128)(2,1)S(1)}, u32[]{:S(2)}, u32[]{:S(2)}) collective-permute-start(bf16[2,4,32,512]{3,2,1,0:T(8,128)(2,1)S(1)} %get-tuple-element.17.refs_0_), channel_id=1, source_target_pairs={{0,12},{1,13},{2,14},{3,15},{4,0},{5,1},{6,2},{7,3},{8,4},{9,5},{1... | collective-permute-start | bytes 786440 | tf_op jit(solution)/shard_map/ppermute | solution.py:479
  32.8 1.0 %copy-start = (bf16[2,128,512]{2,1,0:T(8,128)(2,1)S(1)}, bf16[2,128,512]{2,1,0:T(8,128)(2,1)}, u32[]{:S(2)}) copy-start(bf16[2,128,512]{2,1,0:T(8,128)(2,1)} %get-tuple-element.13.refs_0_) | copy-start | bytes 786436
  35.3 19.9 %all-to-all-start.1 = ((bf16[32,16,512]{2,1,0:T(8,128)(2,1)}), bf16[32,16,512]{2,1,0:T(8,128)(2,1)S(1)}, u32[]{:S(2)}, u32[]{:S(2)}) async-start(bf16[32,16,512]{2,1,0:T(8,128)(2,1)} %bitcast.2), calls=%async_computation.1 | async-start | bytes 1048576 | tf_op jit(solution)/shard_map/all_to_all | solution.py:499
  44.2 0.7 %copy-start.4 = (bf16[2,4,32,512]{3,2,1,0:T(8,128)(2,1)}, bf16[2,4,32,512]{3,2,1,0:T(8,128)(2,1)S(1)}, u32[]{:S(2)}) copy-start(bf16[2,4,32,512]{3,2,1,0:T(8,128)(2,1)S(1)} %collective-permute-done.3.refs_1_) | copy-start | bytes 786436
  44.2 0.8 %copy-start.5 = (bf16[2,4,32,512]{3,2,1,0:T(8,128)(2,1)}, bf16[2,4,32,512]{3,2,1,0:T(8,128)(2,1)S(1)}, u32[]{:S(2)}) copy-start(bf16[2,4,32,512]{3,2,1,0:T(8,128)(2,1)S(1)} %collective-permute-done.4.refs_2_) | copy-start | bytes 786436
  44.3 0.8 %copy-start.6 = (bf16[2,4,32,512]{3,2,1,0:T(8,128)(2,1)}, bf16[2,4,32,512]{3,2,1,0:T(8,128)(2,1)S(1)}, u32[]{:S(2)}) copy-start(bf16[2,4,32,512]{3,2,1,0:T(8,128)(2,1)S(1)} %collective-permute-done.5.refs_3_) | copy-start | bytes 786436
  45.1 10.1 %copy-start.2 = (s32[2,8]{1,0:T(2,128)S(1)}, s32[2,8]{1,0:T(2,128)}, u32[]{:S(2)}) copy-start(s32[2,8]{1,0:T(2,128)} %offsets.9) | copy-start | bytes 196

commit v4 on v3

--- a/solution.py
+++ b/solution.py
@@ -342,17 +342,16 @@
     return moves
 
 
-def choose_kernel(offsets, incoming, out, token):
+def choose_kernel(offsets, incoming, mine, out, held):
     rounds, span = out.shape[:2]
     own = lax.axis_index("tile")
     for q in range(rounds):
         for k in range(span):
             out[q, k] = incoming[(offsets[q, own] + k) % incoming.shape[0], q]
-    token[...] = jnp.zeros_like(token)
-
-
-def near_kernel(offsets, token, *refs):
-    del token
+    held[...] = mine[...]
+
+
+def near_kernel(offsets, *refs):
     landed, out, scratch = refs[:-2], refs[-2], refs[-1]
     groups = out.shape[0]
     rounds, span, far, share, side = scratch.shape
@@ -467,19 +466,19 @@
         name="map_terms",
     )(offsets, turn_counts, map_tiles, sweeps, cotangents, down, across, back, up_sent)
     incoming = lax.all_to_all(outgoing, "tile", split_axis=0, concat_axis=0, tiled=True)
-    kept, token = pl.pallas_call(
+    kept, held = pl.pallas_call(
         choose_kernel,
-        out_shape=[shape((rounds, span, part_rows, side), BF), shape((8, 128), F32)],
-        in_specs=[SMEM, VMEM],
+        out_shape=[shape((rounds, span, part_rows, side), BF), shape(sent[0].shape, BF)],
+        in_specs=[SMEM, VMEM, VMEM],
         out_specs=[VMEM] * 2,
         compiler_params=SMALL,
         name="choose",
-    )(offsets, incoming)
+    )(offsets, incoming, sent[0])
     quarters = [kept] + [
         lax.ppermute(kept, "sweep", [(m, (m + shift * near) % members) for m in range(members)])
         for shift in range(1, far)
     ]
-    landed = [sent[0]]
+    landed = [held]
     for shift in range(1, near):
         pairs = [(m, m // near * near + (m + shift) % near) for m in range(members)]
         landed.append(lax.ppermute(sent[shift], "sweep", pairs))
@@ -487,12 +486,12 @@
     placed = pl.pallas_call(
         near_kernel,
         out_shape=shape((groups, far, rounds * share, side), BF),
-        in_specs=[SMEM, VMEM] + [VMEM] * near,
+        in_specs=[SMEM] + [VMEM] * near,
         out_specs=VMEM,
         scratch_shapes=[pltpu.VMEM((rounds, span, far, share, side), F32)],
         compiler_params=SMALL,
         name="near_sum",
-    )(offsets, token, *landed)
+    )(offsets, *landed)
     index_groups = [
         [t * members + f * near + y for t in range(groups) for f in range(far)] for y in range(near)
     ]

time: 57 us -> 56 us (0.982)
    all_to_all x1, starting transfers between devices: 8.88 us -> 8.26 us  [shards(): lax.all_to_all(placed.reshape(groups * far, rounds * share, side), ('tile...]
  transfers between devices with their start and end apart: 8 -> 8, of which waited for: 3 -> 3; matrix products, arithmetic and copies ran while one was open for 0% -> 0% of each run, Pallas kernels for 18% -> 19%
where the time goes in v4:
time: 56 us; the launch traced here: 55.7 us
  starting transfers between devices  24.9 us (44%)
  Pallas kernels  21.9 us (39%)
  waiting for transfers between devices  6.47 us (12%)
  local copies, waits for them, and re-layouts  1.75 us (3%)
  between operations  0.7 us (1%)
    pallas_call x1, Pallas kernels, shards(): pl.pallas_call(map_kernel, grid=(rounds,), out_shape=[shape((groups, roun...  10.1 us
    all_to_all x1, starting transfers between devices, shards(): lax.all_to_all(placed.reshape(groups * far, rounds * share, side), ('tile...  8.26 us
    pallas_call x1, Pallas kernels, shards(): pl.pallas_call(partial(sweep_kernel, far), grid=(rounds,), out_shape=shap...  8.23 us
    all_to_all x1, starting transfers between devices, shards(): lax.all_to_all(outgoing, 'tile', split_axis=0, concat_axis=0, tiled=True)  5.83 us
    ppermute x3, starting transfers between devices, shards(): lax.ppermute(kept, 'sweep', [(m, (m + shift * near) % members) for m in r...  5.76 us
    ppermute x3, starting transfers between devices, shards(): landed.append(lax.ppermute(sent[shift], 'sweep', pairs))  5.01 us
    all_to_all x1, waiting for transfers between devices, shards(): lax.all_to_all(outgoing, 'tile', split_axis=0, concat_axis=0, tiled=True)  4.47 us
    unnamed x14, local copies, waits for them, and re-layouts  1.75 us
  transfers between devices with their start and end apart: 8, of which 3 were waited for; matrix products, arithmetic and copies ran while one was open for 0% of the time, Pallas kernels for 19%

profile of v4, /device:TPU:1, one launch (start us, length us, event | category | flops | bytes accessed | tf_op | source)
XLA Modules:
  0.0 55.7 jit_solution(14480907623403912595)
XLA Ops:
  0.6 0.0 copy-start.1
  0.6 10.1 %map_terms.1 = (bf16[8,2,32,512]{3,2,1,0:T(8,128)(2,1)}, bf16[2,2,512,512]{3,2,1,0:T(8,128)(2,1)}, f32[2,2,2,8,512]{4,3,2,1,0:T(8,128)}, bf16[2,128,512]{2,1,0:T...) custom-call(s32[2,8]{1,0:T(2,128)} %offsets.9, ...), custom_call_target="tpu_custom_call" | custom-call | flops 4294967296 | bytes 8388608 | tf_op jit(solution)/shard_map/map_terms/pallas_call | solution.py:423
  10.7 5.8 %all-to-all-start = ((bf16[8,2,32,512]{3,2,1,0:T(8,128)(2,1)}), bf16[8,2,32,512]{3,2,1,0:T(8,128)(2,1)S(1)}, u32[]{:S(2)}, u32[]{:S(2)}) async-start(bf16[8,2,32,512]{3,2,1,0:T(8,128)(2,1)} %get-tuple-element.11), calls=%async_computation | async-start | bytes 1048576 | tf_op jit(solution)/shard_map/all_to_all | solution.py:468
  16.5 1.3 %collective-permute-start = (bf16[2,128,512]{2,1,0:T(8,128)(2,1)}, bf16[2,128,512]{2,1,0:T(8,128)(2,1)S(1)}, u32[]{:S(2)}, u32[]{:S(2)}) collective-permute-start(bf16[2,128,512]{2,1,0:T(8,128)(2,1)} %get-tuple-element.14), channel_id=1, source_target_pairs={{0,1},{1,2},{2,3},{3,0},{4,5},{5,6},{6,7},{7,4},{8,9},{9,10},{10,1... | collective-permute-start | bytes 786440 | tf_op jit(solution)/shard_map/ppermute | solution.py:484
  17.8 2.6 %collective-permute-start.1 = (bf16[2,128,512]{2,1,0:T(8,128)(2,1)}, bf16[2,128,512]{2,1,0:T(8,128)(2,1)S(1)}, u32[]{:S(2)}, u32[]{:S(2)}) collective-permute-start(bf16[2,128,512]{2,1,0:T(8,128)(2,1)} %get-tuple-element.15), channel_id=1, source_target_pairs={{0,2},{1,3},{2,0},{3,1},{4,6},{5,7},{6,4},{7,5},{8,10},{9,11},{10,... | collective-permute-start | bytes 786440 | tf_op jit(solution)/shard_map/ppermute | solution.py:484
  20.4 1.1 %collective-permute-start.2 = (bf16[2,128,512]{2,1,0:T(8,128)(2,1)}, bf16[2,128,512]{2,1,0:T(8,128)(2,1)S(1)}, u32[]{:S(2)}, u32[]{:S(2)}) collective-permute-start(bf16[2,128,512]{2,1,0:T(8,128)(2,1)} %get-tuple-element.16), channel_id=1, source_target_pairs={{0,3},{1,0},{2,1},{3,2},{4,7},{5,4},{6,5},{7,6},{8,11},{9,8},{10,9... | collective-permute-start | bytes 786440 | tf_op jit(solution)/shard_map/ppermute | solution.py:484
  21.5 4.5 %all-to-all-done.incoming = bf16[8,2,32,512]{3,2,1,0:T(8,128)(2,1)S(1)} async-done(((bf16[8,2,32,512]{3,2,1,0:T(8,128)(2,1)}), bf16[8,2,32,512]{3,2,1,0:T(8,128)(2,1)S(1)}, u32[]{:S(2)}, u32[]{:S(2)}) %all-to-all-start) | async-done | bytes 524320 | tf_op jit(solution)/shard_map/all_to_all | solution.py:468
  26.0 0.0 copy-done.1
  26.0 0.0 copy-start
  26.0 0.9 %copy-done = bf16[2,128,512]{2,1,0:T(8,128)(2,1)S(1)} copy-done((bf16[2,128,512]{2,1,0:T(8,128)(2,1)S(1)}, bf16[2,128,512]{2,1,0:T(8,128)(2,1)}, u32[]{:S(2)}) %copy-start) | copy-done | bytes 262168
  27.0 0.6 %choose.1 = (bf16[2,4,32,512]{3,2,1,0:T(8,128)(2,1)S(1)}, bf16[2,128,512]{2,1,0:T(8,128)(2,1)S(1)}) custom-call(s32[2,8]{1,0:T(2,128)S(1)} %copy-done.1, bf16[8,2,32,512]{3,2,1,0:T(8,128)(2,1)S(1)} %all-to-all-done.incoming, bf16[2,128,512]{2,1,0:T(8,128)(2,1)S(1)} %copy-done), custom_call_target="tpu_custom_call" | custom-call | tf_op jit(solution)/shard_map/choose/pallas_call | solution.py:469
  27.6 0.0 copy-start.3
  27.6 1.7 %collective-permute-start.3 = (bf16[2,4,32,512]{3,2,1,0:T(8,128)(2,1)S(1)}, bf16[2,4,32,512]{3,2,1,0:T(8,128)(2,1)S(1)}, u32[]{:S(2)}, u32[]{:S(2)}) collective-permute-start(bf16[2,4,32,512]{3,2,1,0:T(8,128)(2,1)S(1)} %get-tuple-element.17.refs_0_), channel_id=1, source_target_pairs={{0,4},{1,5},{2,6},{3,7},{4,8},{5,9},{6,10},{7,11},{8,12},{9,13},{1... | collective-permute-start | bytes 786440 | tf_op jit(solution)/shard_map/ppermute | solution.py:478
  29.3 3.3 %collective-permute-start.4 = (bf16[2,4,32,512]{3,2,1,0:T(8,128)(2,1)S(1)}, bf16[2,4,32,512]{3,2,1,0:T(8,128)(2,1)S(1)}, u32[]{:S(2)}, u32[]{:S(2)}) collective-permute-start(bf16[2,4,32,512]{3,2,1,0:T(8,128)(2,1)S(1)} %get-tuple-element.17.refs_0_), channel_id=1, source_target_pairs={{0,8},{1,9},{2,10},{3,11},{4,12},{5,13},{6,14},{7,15},{8,0},{9,1},... | collective-permute-start | bytes 786440 | tf_op jit(solution)/shard_map/ppermute | solution.py:478
  32.6 0.0 collective-permute-done.refs_1_
  32.6 0.8 %collective-permute-start.5 = (bf16[2,4,32,512]{3,2,1,0:T(8,128)(2,1)S(1)}, bf16[2,4,32,512]{3,2,1,0:T(8,128)(2,1)S(1)}, u32[]{:S(2)}, u32[]{:S(2)}) collective-permute-start(bf16[2,4,32,512]{3,2,1,0:T(8,128)(2,1)S(1)} %get-tuple-element.17.refs_0_), channel_id=1, source_target_pairs={{0,12},{1,13},{2,14},{3,15},{4,0},{5,1},{6,2},{7,3},{8,4},{9,5},{1... | collective-permute-start | bytes 786440 | tf_op jit(solution)/shard_map/ppermute | solution.py:478
  33.3 0.0 collective-permute-done.1.refs_2_
  33.4 0.0 collective-permute-done.2.refs_3_
  33.4 1.6 %near_sum.1 = bf16[8,4,16,512]{3,2,1,0:T(8,128)(2,1)} custom-call(s32[2,8]{1,0:T(2,128)S(1)} %copy-done.1, bf16[2,128,512]{2,1,0:T(8,128)(2,1)S(1)} %get-tuple-element.13.refs_0_, bf16[2,128,512]{2,1,0:T(8,128)(2,1)S(1)} %collective-permute-done.refs_1_, bf16[2,128,512]{2,1,0:T(8,128)(2,1)S(1)} %collective-permute-done.1.refs_2_, ...), custom_call_target="tpu_custom_call" | custom-call | tf_op jit(solution)/shard_map/near_sum/pallas_call | solution.py:486
  35.0 8.3 %all-to-all-start.1 = ((bf16[32,16,512]{2,1,0:T(8,128)(2,1)}), bf16[32,16,512]{2,1,0:T(8,128)(2,1)S(1)}, u32[]{:S(2)}, u32[]{:S(2)}) async-start(bf16[32,16,512]{2,1,0:T(8,128)(2,1)} %bitcast.2), calls=%async_computation.1 | async-start | bytes 1048576 | tf_op jit(solution)/shard_map/all_to_all | solution.py:498
  43.2 0.0 collective-permute-done.3.refs_1_
  43.2 0.0 copy-start.4
  43.3 0.4 collective-permute-done.4.refs_2_
  43.7 0.0 copy-start.5
  43.7 0.0 collective-permute-done.5.refs_3_
  43.7 0.0 copy-start.6
  43.7 0.0 copy-done.3
  43.7 0.3 copy-done.4
  44.0 0.4 copy-done.5
  44.4 0.1 copy-done.6
  44.5 0.0 copy-start.2
  44.5 8.2 %sweep_terms.1 = f32[2,1,512,512]{3,2,1,0:T(8,128)} custom-call(s32[2,8]{1,0:T(2,128)} %offsets.9, s32[2,1,2]{2,1,0:T(1,128)} %turns.3, bf16[2,4,32,512]{3,2,1,0:T(8,128)(2,1)} %copy-done.3, bf16[2,4,32,512]{3,2,1,0:T(8,128)(2,1)} %copy-done.4, bf16[2,4,32,512]{3,2,1,0:T(8,128)(2,1)} %copy-done.5, bf16[2,4,32,512]{3,2,1,0:T(8,128)(2,1)} %copy-done.6, ...), custom_call_target="tpu_custom_call" | custom-call | flops 2684354560 | bytes 8388608 | tf_op jit(solution)/shard_map/sweep_terms/pallas_call | solution.py:515
  52.7 1.6 %all-to-all-done.1 = bf16[32,16,512]{2,1,0:T(8,128)(2,1)S(1)} async-done(((bf16[32,16,512]{2,1,0:T(8,128)(2,1)}), bf16[32,16,512]{2,1,0:T(8,128)(2,1)S(1)}, u32[]{:S(2)}, u32[]{:S(2)}) %all-to-all-start.1) | async-done | bytes 524320 | tf_op jit(solution)/shard_map/all_to_all | solution.py:498
  54.3 0.0 copy-done.2
  54.3 1.4 %gather.1 = f32[16,8,512]{2,1,0:T(8,128)} custom-call(s32[2,8]{1,0:T(2,128)S(1)} %copy-done.2, bf16[8,4,16,512]{3,2,1,0:T(8,128)(2,1)S(1)} %bitcast.4), custom_call_target="tpu_custom_call" | custom-call | tf_op jit(solution)/shard_map/gather/pallas_call | solution.py:506
Async XLA Ops:
  0.6 25.4 %copy-start.1 = (s32[2,8]{1,0:T(2,128)S(1)}, s32[2,8]{1,0:T(2,128)}, u32[]{:S(2)}) copy-start(s32[2,8]{1,0:T(2,128)} %offsets.9) | copy-start | bytes 196
  10.7 15.3 %all-to-all-start = ((bf16[8,2,32,512]{3,2,1,0:T(8,128)(2,1)}), bf16[8,2,32,512]{3,2,1,0:T(8,128)(2,1)S(1)}, u32[]{:S(2)}, u32[]{:S(2)}) async-start(bf16[8,2,32,512]{3,2,1,0:T(8,128)(2,1)} %get-tuple-element.11), calls=%async_computation | async-start | bytes 1048576 | tf_op jit(solution)/shard_map/all_to_all | solution.py:468
  16.5 16.1 %collective-permute-start = (bf16[2,128,512]{2,1,0:T(8,128)(2,1)}, bf16[2,128,512]{2,1,0:T(8,128)(2,1)S(1)}, u32[]{:S(2)}, u32[]{:S(2)}) collective-permute-start(bf16[2,128,512]{2,1,0:T(8,128)(2,1)} %get-tuple-element.14), channel_id=1, source_target_pairs={{0,1},{1,2},{2,3},{3,0},{4,5},{5,6},{6,7},{7,4},{8,9},{9,10},{10,1... | collective-permute-start | bytes 786440 | tf_op jit(solution)/shard_map/ppermute | solution.py:484
  17.8 15.5 %collective-permute-start.1 = (bf16[2,128,512]{2,1,0:T(8,128)(2,1)}, bf16[2,128,512]{2,1,0:T(8,128)(2,1)S(1)}, u32[]{:S(2)}, u32[]{:S(2)}) collective-permute-start(bf16[2,128,512]{2,1,0:T(8,128)(2,1)} %get-tuple-element.15), channel_id=1, source_target_pairs={{0,2},{1,3},{2,0},{3,1},{4,6},{5,7},{6,4},{7,5},{8,10},{9,11},{10,... | collective-permute-start | bytes 786440 | tf_op jit(solution)/shard_map/ppermute | solution.py:484
  20.4 12.9 %collective-permute-start.2 = (bf16[2,128,512]{2,1,0:T(8,128)(2,1)}, bf16[2,128,512]{2,1,0:T(8,128)(2,1)S(1)}, u32[]{:S(2)}, u32[]{:S(2)}) collective-permute-start(bf16[2,128,512]{2,1,0:T(8,128)(2,1)} %get-tuple-element.16), channel_id=1, source_target_pairs={{0,3},{1,0},{2,1},{3,2},{4,7},{5,4},{6,5},{7,6},{8,11},{9,8},{10,9... | collective-permute-start | bytes 786440 | tf_op jit(solution)/shard_map/ppermute | solution.py:484
  26.0 1.0 %copy-start = (bf16[2,128,512]{2,1,0:T(8,128)(2,1)S(1)}, bf16[2,128,512]{2,1,0:T(8,128)(2,1)}, u32[]{:S(2)}) copy-start(bf16[2,128,512]{2,1,0:T(8,128)(2,1)} %get-tuple-element.12.mine) | copy-start | bytes 786436
  27.6 16.1 %copy-start.3 = (bf16[2,4,32,512]{3,2,1,0:T(8,128)(2,1)}, bf16[2,4,32,512]{3,2,1,0:T(8,128)(2,1)S(1)}, u32[]{:S(2)}) copy-start(bf16[2,4,32,512]{3,2,1,0:T(8,128)(2,1)S(1)} %get-tuple-element.17.refs_0_) | copy-start | bytes 786436
  27.6 15.7 %collective-permute-start.3 = (bf16[2,4,32,512]{3,2,1,0:T(8,128)(2,1)S(1)}, bf16[2,4,32,512]{3,2,1,0:T(8,128)(2,1)S(1)}, u32[]{:S(2)}, u32[]{:S(2)}) collective-permute-start(bf16[2,4,32,512]{3,2,1,0:T(8,128)(2,1)S(1)} %get-tuple-element.17.refs_0_), channel_id=1, source_target_pairs={{0,4},{1,5},{2,6},{3,7},{4,8},{5,9},{6,10},{7,11},{8,12},{9,13},{1... | collective-permute-start | bytes 786440 | tf_op jit(solution)/shard_map/ppermute | solution.py:478
  29.3 14.4 %collective-permute-start.4 = (bf16[2,4,32,512]{3,2,1,0:T(8,128)(2,1)S(1)}, bf16[2,4,32,512]{3,2,1,0:T(8,128)(2,1)S(1)}, u32[]{:S(2)}, u32[]{:S(2)}) collective-permute-start(bf16[2,4,32,512]{3,2,1,0:T(8,128)(2,1)S(1)} %get-tuple-element.17.refs_0_), channel_id=1, source_target_pairs={{0,8},{1,9},{2,10},{3,11},{4,12},{5,13},{6,14},{7,15},{8,0},{9,1},... | collective-permute-start | bytes 786440 | tf_op jit(solution)/shard_map/ppermute | solution.py:478
  32.6 11.1 %collective-permute-start.5 = (bf16[2,4,32,512]{3,2,1,0:T(8,128)(2,1)S(1)}, bf16[2,4,32,512]{3,2,1,0:T(8,128)(2,1)S(1)}, u32[]{:S(2)}, u32[]{:S(2)}) collective-permute-start(bf16[2,4,32,512]{3,2,1,0:T(8,128)(2,1)S(1)} %get-tuple-element.17.refs_0_), channel_id=1, source_target_pairs={{0,12},{1,13},{2,14},{3,15},{4,0},{5,1},{6,2},{7,3},{8,4},{9,5},{1... | collective-permute-start | bytes 786440 | tf_op jit(solution)/shard_map/ppermute | solution.py:478
  35.0 19.3 %all-to-all-start.1 = ((bf16[32,16,512]{2,1,0:T(8,128)(2,1)}), bf16[32,16,512]{2,1,0:T(8,128)(2,1)S(1)}, u32[]{:S(2)}, u32[]{:S(2)}) async-start(bf16[32,16,512]{2,1,0:T(8,128)(2,1)} %bitcast.2), calls=%async_computation.1 | async-start | bytes 1048576 | tf_op jit(solution)/shard_map/all_to_all | solution.py:498
  43.2 0.7 %copy-start.4 = (bf16[2,4,32,512]{3,2,1,0:T(8,128)(2,1)}, bf16[2,4,32,512]{3,2,1,0:T(8,128)(2,1)S(1)}, u32[]{:S(2)}) copy-start(bf16[2,4,32,512]{3,2,1,0:T(8,128)(2,1)S(1)} %collective-permute-done.3.refs_1_) | copy-start | bytes 786436
  43.7 0.7 %copy-start.5 = (bf16[2,4,32,512]{3,2,1,0:T(8,128)(2,1)}, bf16[2,4,32,512]{3,2,1,0:T(8,128)(2,1)S(1)}, u32[]{:S(2)}) copy-start(bf16[2,4,32,512]{3,2,1,0:T(8,128)(2,1)S(1)} %collective-permute-done.4.refs_2_) | copy-start | bytes 786436
  43.7 0.8 %copy-start.6 = (bf16[2,4,32,512]{3,2,1,0:T(8,128)(2,1)}, bf16[2,4,32,512]{3,2,1,0:T(8,128)(2,1)S(1)}, u32[]{:S(2)}) copy-start(bf16[2,4,32,512]{3,2,1,0:T(8,128)(2,1)S(1)} %collective-permute-done.5.refs_3_) | copy-start | bytes 786436
  44.5 9.8 %copy-start.2 = (s32[2,8]{1,0:T(2,128)S(1)}, s32[2,8]{1,0:T(2,128)}, u32[]{:S(2)}) copy-start(s32[2,8]{1,0:T(2,128)} %offsets.9) | copy-start | bytes 196
